TPU v7x, 128 devices: a whole 4x4x4 slice. The times are simulated.
128 devices in a mesh: seq: 8 (over z, x_lo), user: 16 (over y, x_hi, core).
Axes of the slice: x: 4 (x_hi: 2, x_lo: 2; x = x_hi * 2 + x_lo), y: 4, z: 4, core: 2. Of those that a mesh axis runs over, the one named last changes fastest.
Arguments:
- history: bfloat16 [16, 2048, 1024], P('user', 'seq'), may hold values from -6 to 6
- segment_ids: int32 [16, 2048], P('user', 'seq'), may hold values from 0 to 3, as said below
- w_in: bfloat16 [1024, 4096], replicated, may hold values from -0.1875 to 0.1875
- w_out: bfloat16 [1024, 1024], replicated, may hold values from -0.1875 to 0.1875
- cotangent: bfloat16 [16, 2048, 1024], P('user', 'seq'), may hold values from -6 to 6
Outputs:
- layer_out: bfloat16 [16, 2048, 1024], P('user', 'seq')
- grad_history: bfloat16 [16, 2048, 1024], P('user', 'seq')
- grad_w_in: float32 [1024, 4096], P(('seq', 'user'))
- grad_w_out: float32 [1024, 1024], P(('seq', 'user'))
Inputs may be any that keep to these rules, and one draw needn't show every extreme that they name: `segment_ids`: in each group the ids never fall along places (time order); each user has 1 to 1536 events and one has exactly 1536.
All inputs are finite; a program needn't handle non-finite values.
Results may differ from a plain program's by a relative error of at most 0.0083.
Values may be sent and summed in bfloat16 or wider, within the bound.
No kernel may reach another device: no remote copies, remote signals or barrier semaphores. Data moves between devices by JAX's collectives and lax.ppermute only.
A program may use at most 192 MiB of HBM per device.

v0:
```python
import functools

import jax
import jax.numpy as jnp
from jax import lax
from jax.experimental import pallas as pl
from jax.experimental.pallas import tpu as pltpu
from jax.sharding import PartitionSpec as P

F32 = jnp.float32
BF16 = jnp.bfloat16
EPS = 1e-05
H = 8
HD = 128
NZ, NX = 4, 2
NY, NXH, NC = 4, 2, 2


def seq_perm(dz, dx):
    return [
        (((z + dz) % NZ) * NX + (x ^ dx), z * NX + x) for z in range(NZ) for x in range(NX)
    ]


def user_perm(dy, dh, dc):
    return [
        ((((y + dy) % NY) * NXH + (h ^ dh)) * NC + (c ^ dc), (y * NXH + h) * NC + c)
        for y in range(NY)
        for h in range(NXH)
        for c in range(NC)
    ]


def from_seq(a, dz, dx):
    return lax.ppermute(a, "seq", seq_perm(dz, dx))


def from_user(a, dy, dh, dc):
    return lax.ppermute(a, "user", user_perm(dy, dh, dc))


def from_both(a, dh, dx):
    pairs = []
    for s in range(NZ * NX):
        for u in range(NY * NXH * NC):
            pairs.append(((s ^ dx) * NY * NXH * NC + (u ^ (dh * NC)), s * NY * NXH * NC + u))
    return lax.ppermute(a, ("seq", "user"), pairs)


def step_one(block):
    return {
        (1, 0): from_seq(block, 1, 0),
        (3, 0): from_seq(block, 3, 0),
        (0, 1): from_seq(block, 0, 1),
    }


def step_two(got):
    return {
        (2, 0): from_seq(got[1, 0], 1, 0),
        (3, 1): from_seq(got[0, 1], 3, 0),
        (1, 1): from_seq(got[1, 0], 0, 1),
    }


def step_three(got, a=96, b=176):
    return {
        (2, 1): jnp.concatenate(
            [
                from_seq(got[2, 0][:a], 0, 1),
                from_seq(got[1, 1][a:b], 1, 0),
                from_seq(got[3, 1][b:], 3, 0),
            ],
            axis=0,
        )
    }


def layer_norm(entries):
    centre = jnp.mean(entries, axis=-1, keepdims=True)
    centred = entries - centre
    inverse = lax.rsqrt(jnp.mean(centred * centred, axis=-1, keepdims=True) + EPS)
    return centred * inverse, inverse


def norm_back(normed, inverse, upstream):
    first_term = jnp.mean(upstream, axis=-1, keepdims=True)
    second_term = jnp.mean(upstream * normed, axis=-1, keepdims=True)
    return inverse * (upstream - first_term - normed * second_term)


def dot(a, b):
    return jnp.dot(a, b, preferred_element_type=F32)


def dot_nt(a, b):
    return lax.dot_general(a, b, (((1,), (1,)), ((), ())), preferred_element_type=F32)


def dot_tn(a, b):
    return lax.dot_general(a, b, (((0,), (0,)), ((), ())), preferred_element_type=F32)


LIMIT = 56


def params(limit):
    return pltpu.CompilerParams(vmem_limit_bytes=limit << 20)


def ln_proj_kernel(count, at_ref, *refs):
    w_ref = refs[count]
    normed_ref, act_ref, slope_ref = refs[-3:]
    half = act_ref.shape[2]
    for k in range(count):

        @pl.when(pl.program_id(0) == k)
        def _():
            normed, _ = layer_norm(refs[k][...].astype(F32))
            normed_b = normed.astype(BF16)
            normed_ref[...] = normed_b.T
            projected = dot(normed_b, w_ref[...])
            tanh = jnp.tanh(0.5 * projected)
            sig = 0.5 + 0.5 * tanh
            silu = projected * sig
            act = silu.astype(BF16)
            slope = sig + silu * (1.0 - sig)
            for i in range(2):
                act_ref[i, 0] = act[i * half : (i + 1) * half]
                slope_ref[i, 0] = slope[i * half : (i + 1) * half]


def ln_proj(at, blocks, w_head, outs):
    rows, width = blocks[0].shape
    cols = w_head.shape[1]
    half, shards = rows // 2, NZ * NX
    by_half = pl.BlockSpec((2, 1, half, cols), lambda i, at_ref: (0, at_ref[i], 0, 0))
    in_specs = [pl.BlockSpec((rows, width), lambda i, at_ref: (0, 0))] * len(blocks)
    in_specs.append(pl.BlockSpec((width, cols), lambda i, at_ref: (0, 0)))
    aliases = {}
    if outs:
        in_specs += [pl.BlockSpec(memory_space=pl.ANY)] * 3
        aliases = {len(in_specs) + k - 2: k for k in range(3)}
    return pl.pallas_call(
        functools.partial(ln_proj_kernel, len(blocks)),
        grid_spec=pltpu.PrefetchScalarGridSpec(
            num_scalar_prefetch=1,
            grid=(len(blocks),),
            in_specs=in_specs,
            out_specs=(
                pl.BlockSpec((width, rows), lambda i, at_ref: (0, at_ref[i])),
                by_half,
                by_half,
            ),
        ),
        out_shape=(
            jax.ShapeDtypeStruct((width, rows * shards), BF16),
            jax.ShapeDtypeStruct((2, shards, half, cols), BF16),
            jax.ShapeDtypeStruct((2, shards, half, cols), F32),
        ),
        input_output_aliases=aliases,
        compiler_params=params(LIMIT),
        cost_estimate=pl.CostEstimate(
            flops=2 * rows * width * cols * len(blocks),
            bytes_accessed=3 * len(blocks) << 20,
            transcendentals=rows * cols * len(blocks),
        ),
        name="ln_proj",
    )(at, *blocks, w_head, *outs)


FQ, FK = 512, 512
BQ, BK = 256, 256
SCALE = HD ** (-0.5)


def tile_place(block):
    last = 2 * NZ * NX - 1
    return (block, 0) if block < NZ * NX else (last - block, HD)


def time_rows(ref, first, count, column, columns=1):
    parts = []
    for block in range(first // HD, (first + count) // HD):
        shard, row = tile_place(block)
        parts.append(ref[row // HD, shard, :, column * HD : (column + columns) * HD])
    return parts[0] if len(parts) == 1 else jnp.concatenate(parts, axis=0)


def tiles(length, rows, cols):
    key_row = lax.broadcasted_iota(jnp.int32, (cols, rows), 0)
    query_col = lax.broadcasted_iota(jnp.int32, (1, rows), 1)

    def seen(i, j, start):
        mask = key_row >= start - j
        if j + cols > i:
            mask = mask & (key_row <= query_col + (i - j))
        return mask

    return [(i, range(0, i + rows, cols)) for i in range(0, length, rows)], seen


def forward_kernel(act_ref, head_ref, start_ref, att_ref, gate_ref, gg_ref, stats_ref):
    length = att_ref.shape[1]
    values_t = [time_rows(act_ref, j, FK, 1).T for j in range(0, length, FK)]
    keys = [time_rows(act_ref, j, FK, 3) for j in range(0, length, FK)]
    queries_in, seen = tiles(length, FQ, FK)
    for i, keys_in in queries_in:
        at = slice(i, i + FQ)
        queries = time_rows(act_ref, i, FQ, 2)
        start = start_ref[:, at]
        total = None
        for j in keys_in:
            half = dot_nt(keys[j // FK], queries) * (0.5 * SCALE)
            weights = half + half * jnp.tanh(half)
            weights = jnp.where(seen(i, j, start), weights, 0.0).astype(BF16)
            term = dot(values_t[j // FK], weights)
            total = term if total is None else total + term
        att_ref[:, at] = total
        gate = time_rows(act_ref, i, FQ, 0).T
        parts = []
        for block in range(i // HD, (i + FQ) // HD):
            shard, row = tile_place(block)
            parts.append(head_ref[shard, row : row + HD, :])
        gg = jnp.concatenate(parts, axis=0).T
        gate_ref[:, at] = gate
        gg_ref[:, at] = gg
        grad_mixed = gg.astype(F32) * gate.astype(F32)
        mean = jnp.sum(total, axis=0, keepdims=True) * (1.0 / HD)
        centred = total - mean
        stats_ref[0:1, at] = mean
        stats_ref[1:2, at] = jnp.sum(centred * centred, axis=0, keepdims=True)
        stats_ref[2:3, at] = jnp.sum(grad_mixed, axis=0, keepdims=True)
        stats_ref[3:4, at] = jnp.sum(grad_mixed * centred, axis=0, keepdims=True)


def vmem():
    return pl.BlockSpec(memory_space=pltpu.VMEM)


def smem():
    return pl.BlockSpec(memory_space=pltpu.SMEM)


def forward(act, at_head, start):
    length = start.shape[1]
    return pl.pallas_call(
        forward_kernel,
        in_specs=[vmem()] * 3,
        out_specs=[vmem()] * 4,
        out_shape=(
            jax.ShapeDtypeStruct((HD, length), F32),
            jax.ShapeDtypeStruct((HD, length), BF16),
            jax.ShapeDtypeStruct((HD, length), BF16),
            jax.ShapeDtypeStruct((4, length), F32),
        ),
        compiler_params=params(LIMIT),
        cost_estimate=pl.CostEstimate(
            flops=8 * HD * length * length, bytes_accessed=6 << 20, transcendentals=length * length // 2
        ),
        name="attention_forward",
    )(act, at_head, start)


def mix_kernel(own_ref, one_ref, three_ref, two_ref, att_ref, gate_ref, gg_ref, slope_ref, early_ref, go_ref, got_ref):
    width = H * HD
    heads = [ref[k] for ref in (own_ref, one_ref, three_ref, two_ref) for k in range(NX)]
    mean_all = sum(a[0:1] for a in heads) * (1.0 / H)
    apart = [a[0:1] - mean_all for a in heads]
    spread = sum(a[1:2] for a in heads) + HD * sum(d * d for d in apart)
    inverse = lax.rsqrt(spread * (1.0 / width) + EPS)
    first = sum(a[2:3] for a in heads) * (1.0 / width)
    second = inverse * sum(a[3:4] + d * a[2:3] for a, d in zip(heads, apart)) * (1.0 / width)
    gate = gate_ref[...].astype(F32)
    gg = gg_ref[...].astype(F32)
    mixed = (att_ref[...] - mean_all) * inverse
    grad_att = inverse * (gg * gate - first - mixed * second)
    got_ref[...] = grad_att.astype(BF16)
    go_ref[...] = grad_att.T.astype(BF16)
    gated = (mixed * gate).astype(BF16).T
    grad_u = (gg * mixed).T
    late = pl.program_id(0) >= NZ * NX // 2

    def put(order):
        for k in range(2):
            at = slice(k * HD, (k + 1) * HD)
            early_ref[order[k], 0, :, :HD] = gated[at]
            early_ref[order[k], 0, :, HD:] = (grad_u[at] * slope_ref[0, order[k]]).astype(BF16)

    pl.when(jnp.logical_not(late))(lambda: put((0, 1)))
    pl.when(late)(lambda: put((1, 0)))


def mix(own, one, three, two, att, gate, gg, slope):
    length = att.shape[1]
    shards = NZ * NX
    tile = 2 * HD
    turn = shards // 2

    def pair(i):
        return jnp.where(i < turn, i, 2 * turn - 1 - i)

    by_tile = pl.BlockSpec((HD, tile), lambda i: (0, i))
    return pl.pallas_call(
        mix_kernel,
        grid=(length // tile,),
        in_specs=[pl.BlockSpec((NX, 4, tile), lambda i: (0, 0, i))] * 4
        + [by_tile] * 3
        + [pl.BlockSpec((1, 2, HD, HD), lambda i: (i // turn, pair(i), 0, 0))],
        out_specs=[
            pl.BlockSpec((2, 1, HD, tile), lambda i: (pair(i), i // turn, 0, 0)),
            pl.BlockSpec((tile, HD), lambda i: (i, 0)),
            by_tile,
        ],
        out_shape=(
            jax.ShapeDtypeStruct((shards, 2, HD, tile), BF16),
            jax.ShapeDtypeStruct((length, HD), BF16),
            jax.ShapeDtypeStruct((HD, length), BF16),
        ),
        compiler_params=params(LIMIT),
        cost_estimate=pl.CostEstimate(flops=20 * HD * length, bytes_accessed=6 << 20, transcendentals=0),
        name="mix",
    )(own, one, three, two, att, gate, gg, slope)


def backward_kernel(act_ref, go_ref, got_ref, start_ref, early_ref, slope_hbm, back_ref, dk_ref, dv_ref, slope_ref, sem):
    length = go_ref.shape[0]
    copy = pltpu.make_async_copy(slope_hbm, slope_ref, sem)
    copy.start()
    for shard in range(NZ * NX):
        for k in range(2):
            rows = slice(k * HD, (k + 1) * HD)
            back_ref[shard, rows, :HD] = early_ref[shard, k, :, HD:]
            back_ref[shard, rows, 4 * HD :] = early_ref[shard, k, :, :HD]
    keys = [time_rows(act_ref, j, BK, 3) for j in range(0, length, BK)]
    keys_t = [k.T for k in keys]
    values = [time_rows(act_ref, j, BK, 1) for j in range(0, length, BK)]
    queries_in, seen = tiles(length, BQ, BK)

    def put(first, column, value):
        value = (value * time_rows(slope_ref, first, value.shape[0], column)).astype(BF16)
        for k in range(value.shape[0] // HD):
            shard, row = tile_place(first // HD + k)
            back_ref[shard, row : row + HD, column * HD : (column + 1) * HD] = value[
                k * HD : (k + 1) * HD
            ]

    started = set()
    for i, keys_in in queries_in:
        at = slice(i, i + BQ)
        queries = time_rows(act_ref, i, BQ, 2)
        grad_out = go_ref[at, :]
        grad_out_t = got_ref[:, at]
        start = start_ref[:, at]
        total = None
        for j in keys_in:
            here = slice(j, j + BK)
            half = dot_nt(keys[j // BK], queries) * (0.5 * SCALE)
            tanh = jnp.tanh(half)
            weights = half + half * tanh
            sig = 0.5 + 0.5 * tanh
            slope = sig + weights * (1.0 - sig)
            mask = seen(i, j, start)
            ahead = dot(values[j // BK], grad_out_t)
            weights = jnp.where(mask, weights, 0.0).astype(BF16)
            slopes = jnp.where(mask, ahead * slope, 0.0).astype(BF16)
            dv = dot(weights, grad_out)
            dk = dot(slopes, queries)
            if j in started:
                dv_ref[here, :] += dv
                dk_ref[here, :] += dk
            else:
                dv_ref[here, :] = dv
                dk_ref[here, :] = dk
                started.add(j)
            term = dot(keys_t[j // BK], slopes)
            total = term if total is None else total + term
        if i == 0:
            copy.wait()
        put(i, 2, total.T * SCALE)
    for j in range(0, length, BK):
        put(j, 1, dv_ref[j : j + BK, :])
        put(j, 3, dk_ref[j : j + BK, :] * SCALE)


def backward(act, grad_out, grad_out_t, start, early, slope):
    length = start.shape[1]
    shards = NZ * NX
    return pl.pallas_call(
        backward_kernel,
        in_specs=[vmem()] * 5 + [pl.BlockSpec(memory_space=pl.ANY)],
        out_specs=vmem(),
        out_shape=jax.ShapeDtypeStruct((shards, length // shards, 5 * HD), BF16),
        scratch_shapes=[pltpu.VMEM((length, HD), F32)] * 2
        + [pltpu.VMEM(slope.shape, F32), pltpu.SemaphoreType.DMA],
        compiler_params=params(LIMIT),
        cost_estimate=pl.CostEstimate(
            flops=15 * HD * length * length, bytes_accessed=10 << 20, transcendentals=length * length // 2
        ),
        name="attention_backward",
    )(act, grad_out, grad_out_t, start, early, slope)


def terms_in_kernel(core_ref, normed_ref, grad_ref, keep_ref, send_ref, res_ref):
    shards, rows, cols = grad_ref.shape
    res_ref[...] = dot(normed_ref[...], grad_ref[...].reshape(shards * rows, cols))
    core = core_ref[0]
    for k in range(res_ref.shape[0] // HD):
        for pair in range(NY * NXH):
            mine = pl.multiple_of(k * HD + (pair * NC + core) * 8, 8)
            other = pl.multiple_of(k * HD + (pair * NC + 1 - core) * 8, 8)
            keep_ref[pair, k * 8 : (k + 1) * 8, :] = res_ref[pl.ds(mine, 8), :]
            send_ref[pair, k * 8 : (k + 1) * 8, :] = res_ref[pl.ds(other, 8), :]


def terms_in(core, normed_t, back):
    width, length = normed_t.shape
    shards, rows, _ = back.shape
    shape = jax.ShapeDtypeStruct((NY * NXH, 80, 4 * HD), F32)
    out_spec = pl.BlockSpec((NY * NXH, 16, 4 * HD), lambda g: (0, g, 0))
    return pl.pallas_call(
        terms_in_kernel,
        grid=(4,),
        in_specs=[
            smem(),
            pl.BlockSpec((width // 4, length), lambda g: (g, 0)),
            pl.BlockSpec((shards, rows, 4 * HD), lambda g: (0, 0, 0)),
        ],
        out_specs=[out_spec] * 2,
        out_shape=[shape] * 2,
        scratch_shapes=[pltpu.VMEM((width // 4, 4 * HD), F32)],
        compiler_params=params(LIMIT),
        cost_estimate=pl.CostEstimate(
            flops=2 * width * length * 4 * HD, bytes_accessed=9 << 20, transcendentals=0
        ),
        name="terms_in",
    )(core, normed_t, back)


def terms_out_kernel(core_ref, gated_ref, cot_ref, _, __, keep_ref, send_ref, res_ref, gated_t_ref):
    shards, rows, _ = gated_ref.shape

    @pl.when(pl.program_id(0) == 0)
    def _():
        for shard in range(shards):
            gated_t_ref[:, shard * rows : (shard + 1) * rows] = gated_ref[shard].T

    res_ref[...] = dot(gated_t_ref[...], cot_ref[...])
    core = core_ref[0]
    for pair in range(NY * NXH):
        for out_ref, who in ((keep_ref, core), (send_ref, 1 - core)):
            out_ref[pair] = res_ref[pl.ds(pl.multiple_of((pair * NC + who) * 8, 8), 8), :]


def terms_out(core, back, cot_all, keep, send):
    shards, rows, _ = back.shape
    length, width = cot_all.shape
    out_spec = pl.BlockSpec((NY * NXH, 8, 4 * HD), lambda g: (0, 8 + g, 0))
    return pl.pallas_call(
        terms_out_kernel,
        grid=(2,),
        in_specs=[
            smem(),
            pl.BlockSpec((shards, rows, HD), lambda g: (0, 0, 4)),
            pl.BlockSpec((length, width // 2), lambda g: (0, g)),
        ]
        + [pl.BlockSpec(memory_space=pl.ANY)] * 2,
        out_specs=[out_spec] * 2,
        out_shape=[jax.ShapeDtypeStruct(keep.shape, F32)] * 2,
        scratch_shapes=[pltpu.VMEM((HD, width // 2), F32), pltpu.VMEM((HD, length), BF16)],
        input_output_aliases={3: 0, 4: 1},
        compiler_params=params(LIMIT),
        cost_estimate=pl.CostEstimate(
            flops=2 * HD * width * length, bytes_accessed=6 << 20, transcendentals=0
        ),
        name="terms_out",
    )(core, back, cot_all, keep, send)


def small(kernel, name, scalars, arrays, outs, scratch=(), limit=12):
    size = sum(a.size * a.dtype.itemsize for a in arrays)
    return pl.pallas_call(
        kernel,
        in_specs=[smem()] + [vmem()] * len(arrays),
        out_specs=[vmem()] * len(outs),
        out_shape=[jax.ShapeDtypeStruct(shape, dtype) for shape, dtype in outs],
        scratch_shapes=list(scratch),
        compiler_params=params(limit),
        cost_estimate=pl.CostEstimate(flops=size, bytes_accessed=2 * size, transcendentals=0),
        name=name,
    )(scalars, *arrays)


def core_sum_kernel(pos_ref, keep_ref, got_ref, own_ref, one_ref, three_ref, two_ref):
    y = pos_ref[0]
    for d, out_ref in ((0, own_ref), (1, one_ref), (3, three_ref), (2, two_ref)):
        here = pl.ds(((y - d + NY) % NY) * NXH, NXH)
        out_ref[...] = (keep_ref[here] + got_ref[here]).astype(out_ref.dtype)


def y_sum_kernel(pos_ref, own_ref, a_ref, b_ref, c_ref, keep_ref, same_ref, one_ref, two_ref, sum_ref):
    xh, x = pos_ref[1], pos_ref[2]
    sum_ref[...] = own_ref[...] + (
        a_ref[...].astype(F32) + b_ref[...].astype(F32) + c_ref[...].astype(F32)
    )

    def slab(out_ref, h, l):
        for k in range(NZ):
            out_ref[k * 8 : (k + 1) * 8, :] = sum_ref[
                h, pl.ds(pl.multiple_of((k * NX + l) * 8, 8), 8), :
            ]

    slab(keep_ref, xh, x)
    keep_ref[32:, :] = sum_ref[xh, 64:, :]
    slab(same_ref, 1 - xh, x)
    same_ref[32:, :] = sum_ref[1 - xh, 64:, :]
    slab(one_ref, xh, 1 - x)
    slab(two_ref, 1 - xh, 1 - x)


def x_sum_kernel(pos_ref, keep_ref, same_ref, a_ref, b_ref, own_ref, one_ref, three_ref, two_ref, out_ref, sum_ref):
    z, x = pos_ref[3], pos_ref[2]
    mine = keep_ref[...] + same_ref[...]
    sum_ref[x] = mine[:32]
    sum_ref[1 - x] = a_ref[...] + b_ref[...]
    out_ref[...] = mine[32:]
    for d, to_ref in ((0, own_ref), (1, one_ref), (3, three_ref), (2, two_ref)):
        here = pl.ds(pl.multiple_of(((z - d + NZ) % NZ) * 8, 8), 8)
        for l in range(NX):
            to_ref[l * 8 : (l + 1) * 8, :] = sum_ref[l, here, :]


def z_place_kernel(factor, pos_ref, own_ref, one_ref, three_ref, two_ref, out_ref, w_in_ref, w_out_ref):
    z = pos_ref[3]
    for d, ref in ((0, own_ref), (1, one_ref), (3, three_ref), (2, two_ref)):
        for l in range(NX):
            for k in range(4):
                at = pl.multiple_of((k * H + ((z + d) % NZ) * NX + l) * HD, HD)
                w_in_ref[:, pl.ds(at, HD)] = (
                    ref[l * 8 : (l + 1) * 8, k * HD : (k + 1) * HD] * factor
                )
    w_out_ref[:, : 4 * HD] = out_ref[:8] * factor
    w_out_ref[:, 4 * HD :] = out_ref[8:] * factor


def shard_kernel(gated_ref, grad_ref, w_in_ref, w_out_ref, hist_ref, cot_ref, layer_ref, grad_hist_ref, acc_ref):
    step = pl.program_id(0)

    def columns(ref):
        return jnp.concatenate([ref[h] for h in range(H)], axis=1)

    term = dot_nt(columns(grad_ref), w_in_ref[...])

    @pl.when(step == 0)
    def _():
        hist = hist_ref[...].astype(F32)
        layer_ref[...] = (hist + dot(columns(gated_ref), w_out_ref[...])).astype(BF16)
        acc_ref[...] = term

    @pl.when(step > 0)
    def _():
        acc_ref[...] += term

    @pl.when(step == 3)
    def _():
        normed, inverse = layer_norm(hist_ref[...].astype(F32))
        grad = norm_back(normed, inverse, acc_ref[...])
        grad_hist_ref[...] = (cot_ref[...].astype(F32) + grad).astype(BF16)


def shard_outputs(back, w_in, w_out, hist, cot):
    rows, width = hist.shape
    whole = lambda a: pl.BlockSpec(a.shape, lambda k: (0,) * a.ndim)
    return pl.pallas_call(
        shard_kernel,
        grid=(4,),
        in_specs=[
            pl.BlockSpec((H, rows, HD), lambda k: (0, 0, 4)),
            pl.BlockSpec((H, rows, HD), lambda k: (0, 0, k)),
            pl.BlockSpec((width, width), lambda k: (0, k)),
            whole(w_out),
            whole(hist),
            whole(cot),
        ],
        out_specs=[whole(hist)] * 2,
        out_shape=[jax.ShapeDtypeStruct(hist.shape, BF16)] * 2,
        scratch_shapes=[pltpu.VMEM((rows, width), F32)],
        compiler_params=params(LIMIT),
        cost_estimate=pl.CostEstimate(
            flops=10 * rows * width * width, bytes_accessed=14 << 20, transcendentals=0
        ),
        name="shard_outputs",
    )(back, back, w_in, w_out, hist, cot)


def local(history, segment_ids, w_in, w_out, cotangent):
    hist = history[0]
    cot = cotangent[0]
    rows, width = hist.shape
    length = rows * NZ * NX
    s = lax.axis_index("seq")
    u = lax.axis_index("user")
    z, x = s // NX, s % NX
    y, xh, core = u // (NXH * NC), (u // NC) % NXH, u % NC

    users = NY * NXH * NC
    tie = lax.optimization_barrier
    w_head = jnp.concatenate(
        [lax.dynamic_slice(w_in, (0, i * width + s * HD), (width, HD)) for i in range(4)], axis=1
    )

    def place_of(key):
        return ((z + key[0]) % NZ) * NX + (x ^ key[1])

    def project(got, outs):
        at = jnp.stack([place_of(key) for key in got])
        return ln_proj(at, list(got.values()), w_head, outs)

    got = step_one(hist)
    outs = project({(0, 0): hist}, ())
    grad_gated_own = dot_nt(cot, w_out).astype(BF16).reshape(rows, H, HD).transpose(1, 0, 2)
    got, outs, grad_gated_own, cot_next = tie((got, outs, grad_gated_own, cot))
    cot_all = lax.all_gather(cot_next, "seq", axis=0, tiled=True)
    ids = segment_ids[0].astype(BF16).reshape(2, HD)
    ids = jnp.pad(ids, ((0, 14), (0, 0)))
    to_heads = jnp.concatenate(
        [
            grad_gated_own,
            jnp.broadcast_to(ids[None], (H, 16, HD)),
        ],
        axis=1,
    )
    at_head = lax.all_to_all(to_heads, "seq", 0, 0, tiled=True)
    more = step_two(got)
    outs = project(got, outs)
    more, outs = tie((more, outs))
    got.update(more)
    last = step_three(got)
    outs = project(more, outs)
    ids = at_head[:, rows : rows + 2].astype(jnp.int32)
    ids = jnp.concatenate([ids[:, 0], ids[::-1, 1]], axis=0).reshape(1, length)
    start = sum(jnp.where(ids > v, jnp.sum((ids == v).astype(jnp.int32)), 0) for v in range(3))
    last, outs, start, at_head = tie((last, outs, start, at_head))
    normed_t, act, slope = project(last, outs)
    att, gate_t, gg_t, stats = forward(act, at_head, start)
    pair = jnp.stack([stats, from_seq(stats, 0, 1)])
    others = [from_seq(pair, dz, 0) for dz in (1, 3, 2)]
    early, grad_out, grad_out_t = mix(pair, *others, att, gate_t, gg_t, slope)
    back = backward(act, grad_out, grad_out_t, start, early, slope)
    back_tok = lax.all_to_all(back, "seq", 0, 0, tiled=True)

    at_core = core.reshape(1)
    keep, send = terms_in(at_core, normed_t, back)
    keep, send = terms_out(at_core, back, cot_all, keep, send)
    at = jnp.stack([y, xh, x, z])
    n = 4 * HD
    got = from_user(send, 0, 0, 1)
    own, *sends = small(
        core_sum_kernel,
        "core_sum",
        at,
        [keep, got],
        [((NXH, 80, n), F32)] + [((NXH, 80, n), BF16)] * 3,
        limit=LIMIT,
    )
    back_tok, own, sends = tie((back_tok, own, sends))
    sends = [from_user(a, d, 0, 0) for a, d in zip(sends, (1, 3, 2))]
    layer_out, grad_history = shard_outputs(back_tok, w_in, w_out, hist, cot)
    sends, layer_out, grad_history = tie((sends, layer_out, grad_history))
    keep, same, one, two = small(
        y_sum_kernel,
        "y_sum",
        at,
        [own, *sends],
        [((48, n), F32)] * 2 + [((32, n), F32)] * 2,
        [pltpu.VMEM((NXH, 80, n), F32)],
    )
    same = from_both(same, 1, 0)
    one = from_both(one, 0, 1)
    two = from_both(two, 1, 1)
    own, *sends, own_out = small(
        x_sum_kernel,
        "x_sum",
        at,
        [keep, same, one, two],
        [((16, n), F32)] * 5,
        [pltpu.VMEM((NX, 32, n), F32)],
    )
    sends = [from_seq(a, d, 0) for a, d in zip(sends, (1, 3, 2))]
    factor = (length * users) ** (-0.5)
    grad_w_in, grad_w_out = small(
        functools.partial(z_place_kernel, factor),
        "z_place",
        at,
        [own, *sends, own_out],
        [((8, 4 * width), F32), ((8, width), F32)],
    )
    return layer_out[None], grad_history[None], grad_w_in, grad_w_out


def solution(mesh):
    in_specs = (P("user", "seq", None), P("user", "seq"), P(), P(), P("user", "seq", None))
    out_specs = (
        P("user", "seq", None),
        P("user", "seq", None),
        P(("seq", "user"), None),
        P(("seq", "user"), None),
    )
    return jax.shard_map(local, mesh=mesh, in_specs=in_specs, out_specs=out_specs, check_vma=False)
```

profile of v0, /device:TPU:0, one launch (start us, length us, event | category | flops | bytes accessed | tf_op | source)
XLA Modules:
  0.0 204.1 jit_solution(17423358333296921136)
XLA Ops:
  7.2 1.7 collective-permute-start
  8.9 4.0 %collective-permute-start.1 = (bf16[256,1024]{1,0:T(8,128)(2,1)}, bf16[256,1024]{1,0:T(8,128)(2,1)S(1)}, u32[]{:S(2)}, u32[]{:S(2)}) collective-permute-start(bf16[256,1024]{1,0:T(8,128)(2,1)} %bitcast.31), channel_id=1, source_target_pairs={{32,0},{48,16},{64,32},{80,48},{96,64},{112,80},{0,96},{16,112},{3... | collective-permute-start | bytes 1572872 | tf_op jit(solution)/shard_map/ppermute | solution.py:35
  12.9 2.5 %convolution_convert_fusion = bf16[256,1024]{1,0:T(8,128)(2,1)S(1)} fusion(bf16[1024,1024]{1,0:T(8,128)(2,1)} %w_out_ref.1, bf16[1,256,1024]{2,1,0:T(8,128)(2,1)} %param.9), kind=kOutput, calls=%fused_computation | convolution fusion | flops 537133056 | bytes 3145728 | tf_op jit(solution)/shard_map/dot_general | solution.py:97
  15.9 1.3 constant_dynamic-slice_fusion.3
  17.2 1.1 pad_maximum_fusion.refs_1_.refs_3_
  18.3 3.1 %ln_proj.4 = (bf16[1024,2048]{1,0:T(8,128)(2,1)}, bf16[2,8,128,512]{3,2,1,0:T(8,128)(2,1)}, f32[2,8,128,512]{3,2,1,0:T(8,128)}) custom-call(s32[1]{0:T(128)} %bitcast.2.at_ref, bf16[256,1024]{1,0:T(8,128)(2,1)} %bitcast.33, bf16[1024,512]{1,0:T(8,128)(2,1)} %pad_maximum_fusion.refs_1_.refs_3_), custom_call_target="tpu_custom_call" | custom-call | flops 268435456 | bytes 3145728 | tf_op jit(solution)/shard_map/ln_proj/pallas_call | solution.py:144
  21.5 2.7 %collective-permute-done.1.refs_1_ = bf16[256,1024]{1,0:T(8,128)(2,1)S(1)} collective-permute-done((bf16[256,1024]{1,0:T(8,128)(2,1)}, bf16[256,1024]{1,0:T(8,128)(2,1)S(1)}, u32[]{:S(2)}, u32[]{:S(2)}) %collective-permute-start.1) | collective-permute-done | bytes 524320 | tf_op jit(solution)/shard_map/ppermute | solution.py:35
  24.1 3.3 %collective-permute-done.2.refs_2_ = bf16[256,1024]{1,0:T(8,128)(2,1)S(1)} collective-permute-done((bf16[256,1024]{1,0:T(8,128)(2,1)}, bf16[256,1024]{1,0:T(8,128)(2,1)S(1)}, u32[]{:S(2)}, u32[]{:S(2)}) %collective-permute-start.2) | collective-permute-done | bytes 524320 | tf_op jit(solution)/shard_map/ppermute | solution.py:35
  27.5 0.9 pad_maximum_fusion.1
  28.4 3.5 %all-to-all-start = ((bf16[8,272,128]{2,1,0:T(8,128)(2,1)}), bf16[8,272,128]{2,1,0:T(8,128)(2,1)S(1)}, u32[]{:S(2)}, u32[]{:S(2)}) async-start(bf16[8,272,128]{2,1,0:T(8,128)(2,1)} %pad_maximum_fusion.1), calls=%async_computation | async-start | bytes 1114112 | tf_op jit(solution)/shard_map/all_to_all | solution.py:633
  32.0 1.9 collective-permute-start.3
  33.9 2.7 %collective-permute-start.4 = (bf16[256,1024]{1,0:T(8,128)(2,1)S(1)}, bf16[256,1024]{1,0:T(8,128)(2,1)S(1)}, u32[]{:S(2)}, u32[]{:S(2)}) collective-permute-start(bf16[256,1024]{1,0:T(8,128)(2,1)S(1)} %collective-permute-done.1.refs_1_), channel_id=1, source_target_pairs={{32,0},{48,16},{64,32},{80,48},{96,64},{112,80},{0,96},{16,112},{3... | collective-permute-start | bytes 1572872 | tf_op jit(solution)/shard_map/ppermute | solution.py:35
  37.2 6.2 %ln_proj.5 = (bf16[1024,2048]{1,0:T(8,128)(2,1)}, bf16[2,8,128,512]{3,2,1,0:T(8,128)(2,1)}, f32[2,8,128,512]{3,2,1,0:T(8,128)}) custom-call(s32[3]{0:T(128)} %get-tuple-element.153.at_ref, bf16[256,1024]{1,0:T(8,128)(2,1)} %copy-done.7, bf16[256,1024]{1,0:T(8,128)(2,1)} %copy-done.8, ...), custom_call_target="tpu_custom_call", output_to_operand_aliasing={{0}: (5, {}), {1}: (6, {}), {2}: (7, {})} | custom-call | flops 805306368 | bytes 9437184 | tf_op jit(solution)/shard_map/ln_proj/pallas_call | solution.py:144
  43.4 5.0 %all-to-all-done.head_ref = bf16[8,272,128]{2,1,0:T(8,128)(2,1)S(1)} async-done(((bf16[8,272,128]{2,1,0:T(8,128)(2,1)}), bf16[8,272,128]{2,1,0:T(8,128)(2,1)S(1)}, u32[]{:S(2)}, u32[]{:S(2)}) %all-to-all-start) | async-done | bytes 557088 | tf_op jit(solution)/shard_map/all_to_all | solution.py:633
  48.5 19.6 %collective-permute-done.3.refs_0_ = bf16[256,1024]{1,0:T(8,128)(2,1)S(1)} collective-permute-done((bf16[256,1024]{1,0:T(8,128)(2,1)S(1)}, bf16[256,1024]{1,0:T(8,128)(2,1)S(1)}, u32[]{:S(2)}, u32[]{:S(2)}) %collective-permute-start.3) | collective-permute-done | bytes 524320 | tf_op jit(solution)/shard_map/ppermute | solution.py:35
  68.3 0.9 convert_reduce_fusion.2
  69.2 2.8 %collective-permute-start.7 = (bf16[80,1024]{1,0:T(8,128)(2,1)S(1)}, bf16[80,1024]{1,0:T(8,128)(2,1)S(1)}, u32[]{:S(2)}, u32[]{:S(2)}) collective-permute-start(bf16[80,1024]{1,0:T(8,128)(2,1)S(1)} %slice.19), channel_id=1, source_target_pairs={{32,0},{48,16},{64,32},{80,48},{96,64},{112,80},{0,96},{16,112},{3... | collective-permute-start | bytes 491528 | tf_op jit(solution)/shard_map/ppermute | solution.py:35
  72.3 2.4 %select_add_fusion = s32[16,128]{1,0:T(8,128)} fusion(s32[]{:T(128)} %get-tuple-element.145, s32[]{:T(128)} %get-tuple-element.146, s32[]{:T(128)} %get-tuple-element.144, s32[8,128]{1,0:T(8,128)S(1)} %bitcast.40, s32[8,128]{1,0:T(8,128)S(1)} %bitcast.42), kind=kLoop, calls=%fused_computation.6 | loop fusion | flops 18432 | bytes 16396 | tf_op jit(solution)/shard_map/add | solution.py:642
  74.7 6.3 %ln_proj.6 = (bf16[1024,2048]{1,0:T(8,128)(2,1)}, bf16[2,8,128,512]{3,2,1,0:T(8,128)(2,1)}, f32[2,8,128,512]{3,2,1,0:T(8,128)}) custom-call(s32[3]{0:T(128)} %get-tuple-element.154.at_ref, bf16[256,1024]{1,0:T(8,128)(2,1)} %copy-done.4, bf16[256,1024]{1,0:T(8,128)(2,1)} %copy-done.3, ...), custom_call_target="tpu_custom_call", output_to_operand_aliasing={{0}: (5, {}), {1}: (6, {}), {2}: (7, {})} | custom-call | flops 805306368 | bytes 9437184 | tf_op jit(solution)/shard_map/ln_proj/pallas_call | solution.py:144
  81.1 0.8 pad_maximum_fusion.2.refs_0_
  81.9 3.1 %ln_proj.7 = (bf16[1024,2048]{1,0:T(8,128)(2,1)}, bf16[2,8,128,512]{3,2,1,0:T(8,128)(2,1)}, f32[2,8,128,512]{3,2,1,0:T(8,128)}) custom-call(s32[1]{0:T(128)} %bitcast.at_ref, bf16[256,1024]{1,0:T(8,128)(2,1)} %pad_maximum_fusion.2.refs_0_, ...), custom_call_target="tpu_custom_call", output_to_operand_aliasing={{0}: (3, {}), {1}: (4, {}), {2}: (5, {})} | custom-call | flops 268435456 | bytes 3145728 | tf_op jit(solution)/shard_map/ln_proj/pallas_call | solution.py:144
  85.0 6.8 %attention_forward.1 = (f32[128,2048]{1,0:T(8,128)}, bf16[128,2048]{1,0:T(8,128)(2,1)}, bf16[128,2048]{1,0:T(8,128)(2,1)}, f32[4,2048]{1,0:T(4,128)}) custom-call(bf16[2,8,128,512]{3,2,1,0:T(8,128)(2,1)} %get-tuple-element.100.act_ref, bf16[8,272,128]{2,1,0:T(8,128)(2,1)} %copy-done.6, s32[1,2048]{1,0:T(1,128)} %bitcast.45), custom_call_target="tpu_custom_call" | custom-call | flops 4294967296 | bytes 6291456 | tf_op jit(solution)/shard_map/attention_forward/pallas_call | solution.py:247
  91.8 1.3 collective-permute-start.9
  93.2 3.5 %collective-permute-done.9 = f32[4,2048]{1,0:T(4,128)S(1)} collective-permute-done((f32[4,2048]{1,0:T(4,128)}, f32[4,2048]{1,0:T(4,128)S(1)}, u32[]{:S(2)}, u32[]{:S(2)}) %collective-permute-start.9) | collective-permute-done | bytes 32800 | tf_op jit(solution)/shard_map/ppermute | solution.py:35
  97.4 3.3 %collective-permute-start.10 = (f32[2,4,2048]{2,1,0:T(4,128)S(1)}, f32[2,4,2048]{2,1,0:T(4,128)S(1)}, u32[]{:S(2)}, u32[]{:S(2)}) collective-permute-start(f32[2,4,2048]{2,1,0:T(4,128)S(1)} %pad_maximum_fusion.3.own_ref), channel_id=1, source_target_pairs={{32,0},{48,16},{64,32},{80,48},{96,64},{112,80},{0,96},{16,112},{3... | collective-permute-start | bytes 196616 | tf_op jit(solution)/shard_map/ppermute | solution.py:35
  100.7 1.5 collective-permute-start.12
  102.6 5.6 %collective-permute-done.11.three_ref = f32[2,4,2048]{2,1,0:T(4,128)S(1)} collective-permute-done((f32[2,4,2048]{2,1,0:T(4,128)S(1)}, f32[2,4,2048]{2,1,0:T(4,128)S(1)}, u32[]{:S(2)}, u32[]{:S(2)}) %collective-permute-start.11) | collective-permute-done | bytes 65568 | tf_op jit(solution)/shard_map/ppermute | solution.py:35
  108.9 7.1 %mix.1 = (bf16[8,2,128,256]{3,2,1,0:T(8,128)(2,1)}, bf16[2048,128]{1,0:T(8,128)(2,1)}, bf16[128,2048]{1,0:T(8,128)(2,1)}) custom-call(f32[2,4,2048]{2,1,0:T(4,128)} %copy-done.10, f32[2,4,2048]{2,1,0:T(4,128)} %copy-done.11, f32[2,4,2048]{2,1,0:T(4,128)} %copy-done.12, f32[2,4,2048]{2,1,0:T(4,128)} %copy-done.13, f32[128,2048]{1,0:T(8,128)} %get-tuple-element.104.att_ref, ...), custom_call_target="tpu_custom_call" | custom-call | flops 5242880 | bytes 6291456 | tf_op jit(solution)/shard_map/mix/pallas_call | solution.py:304
  116.0 15.3 %attention_backward.1.grad_ref.gated_ref = bf16[8,256,640]{2,1,0:T(8,128)(2,1)} custom-call(bf16[2,8,128,512]{3,2,1,0:T(8,128)(2,1)} %get-tuple-element.100.act_ref, bf16[2048,128]{1,0:T(8,128)(2,1)} %get-tuple-element.108.go_ref, bf16[128,2048]{1,0:T(8,128)(2,1)} %get-tuple-element.109.got_ref, s32[1,2048]{1,0:T(1,128)} %bitcast.46, ...), custom_call_target="tpu_custom_call" | custom-call | flops 8053063680 | bytes 10485760 | tf_op jit(solution)/shard_map/attention_backward/pallas_call | solution.py:389
  131.2 4.2 %all-to-all-start.1 = ((bf16[8,256,640]{2,1,0:T(8,128)(2,1)}), bf16[8,256,640]{2,1,0:T(8,128)(2,1)S(1)}, u32[]{:S(2)}, u32[]{:S(2)}) async-start(bf16[8,256,640]{2,1,0:T(8,128)(2,1)} %attention_backward.1.grad_ref.gated_ref), calls=%async_computation.1 | async-start | bytes 5242880 | tf_op jit(solution)/shard_map/all_to_all | solution.py:650
  135.5 6.5 %terms_in.1 = (f32[8,80,512]{2,1,0:T(8,128)}, f32[8,80,512]{2,1,0:T(8,128)}) custom-call(s32[1]{0:T(128)} %bitcast.21.core_ref, bf16[1024,2048]{1,0:T(8,128)(2,1)} %get-tuple-element.112.normed_ref, bf16[8,256,640]{2,1,0:T(8,128)(2,1)} %attention_backward.1.grad_ref.gated_ref), custom_call_target="tpu_custom_call" | custom-call | flops 2147483648 | bytes 9437184 | tf_op jit(solution)/shard_map/terms_in/pallas_call | solution.py:421
  142.0 3.6 %terms_out.1 = (f32[8,80,512]{2,1,0:T(8,128)}, f32[8,80,512]{2,1,0:T(8,128)}) custom-call(s32[1]{0:T(128)} %bitcast.21.core_ref, bf16[8,256,640]{2,1,0:T(8,128)(2,1)} %attention_backward.1.grad_ref.gated_ref, bf16[2048,1024]{1,0:T(8,128)(2,1)} %all-gather.2.cloned.1.call-done.cot_ref, ...), custom_call_target="tpu_custom_call", output_to_operand_aliasing={{0}: (3, {}), {1}: (4, {})} | custom-call | flops 536870912 | bytes 6291456 | tf_op jit(solution)/shard_map/terms_out/pallas_call | solution.py:459
  146.2 2.8 %collective-permute-done.13.got_ref = f32[8,80,512]{2,1,0:T(8,128)} collective-permute-done((f32[8,80,512]{2,1,0:T(8,128)}, f32[8,80,512]{2,1,0:T(8,128)}, u32[]{:S(2)}, u32[]{:S(2)}) %collective-permute-start.13) | collective-permute-done | bytes 1310752 | tf_op jit(solution)/shard_map/ppermute | solution.py:39
  149.0 2.8 %core_sum.1 = (f32[2,80,512]{2,1,0:T(8,128)}, bf16[2,80,512]{2,1,0:T(8,128)(2,1)}, bf16[2,80,512]{2,1,0:T(8,128)(2,1)}, bf16[2,80,512]{2,1,0:T(8,128)(2,1)}) custom-call(s32[4]{0:T(128)} %pad_add_fusion.3.pos_ref, f32[8,80,512]{2,1,0:T(8,128)} %get-tuple-element.115.keep_ref, f32[8,80,512]{2,1,0:T(8,128)} %collective-permute-done.13.got_ref), custom_call_target="tpu_custom_call" | custom-call | flops 2621440 | bytes 5242880 | tf_op jit(solution)/shard_map/core_sum/pallas_call | solution.py:482
  151.8 12.7 %all-to-all-done.1.gated_ref.grad_ref = bf16[8,256,640]{2,1,0:T(8,128)(2,1)S(1)} async-done(((bf16[8,256,640]{2,1,0:T(8,128)(2,1)}), bf16[8,256,640]{2,1,0:T(8,128)(2,1)S(1)}, u32[]{:S(2)}, u32[]{:S(2)}) %all-to-all-start.1) | async-done | bytes 2621472 | tf_op jit(solution)/shard_map/all_to_all | solution.py:650
  164.5 2.6 %collective-permute-start.14 = (bf16[2,80,512]{2,1,0:T(8,128)(2,1)}, bf16[2,80,512]{2,1,0:T(8,128)(2,1)S(1)}, u32[]{:S(2)}, u32[]{:S(2)}) collective-permute-start(bf16[2,80,512]{2,1,0:T(8,128)(2,1)} %get-tuple-element.121), channel_id=1, source_target_pairs={{4,0},{5,1},{6,2},{7,3},{8,4},{9,5},{10,6},{11,7},{12,8},{13,9},{1... | collective-permute-start | bytes 491528 | tf_op jit(solution)/shard_map/ppermute | solution.py:39
  167.1 2.3 %collective-permute-start.16 = (bf16[2,80,512]{2,1,0:T(8,128)(2,1)}, bf16[2,80,512]{2,1,0:T(8,128)(2,1)S(1)}, u32[]{:S(2)}, u32[]{:S(2)}) collective-permute-start(bf16[2,80,512]{2,1,0:T(8,128)(2,1)} %get-tuple-element.123), channel_id=1, source_target_pairs={{8,0},{9,1},{10,2},{11,3},{12,4},{13,5},{14,6},{15,7},{0,8},{1,9},... | collective-permute-start | bytes 491528 | tf_op jit(solution)/shard_map/ppermute | solution.py:39
  169.4 9.6 %shard_outputs.1 = (bf16[256,1024]{1,0:T(8,128)(2,1)}, bf16[256,1024]{1,0:T(8,128)(2,1)}) custom-call(bf16[8,256,640]{2,1,0:T(8,128)(2,1)} %copy-done.2, bf16[8,256,640]{2,1,0:T(8,128)(2,1)} %copy-done.2, bf16[1024,4096]{1,0:T(8,128)(2,1)} %w_in_ref.1, bf16[1024,1024]{1,0:T(8,128)(2,1)} %w_out_ref.1, bf16[256,1024]{1,0:T(8,128)(2,1)} %bitcast.34, ...), custom_call_target="tpu_custom_call" | custom-call | flops 2684354560 | bytes 14680064 | tf_op jit(solution)/shard_map/shard_outputs/pallas_call | solution.py:574
  179.7 2.8 %collective-permute-start.17 = (f32[48,512]{1,0:T(8,128)S(1)}, f32[48,512]{1,0:T(8,128)S(1)}, u32[]{:S(2)}, u32[]{:S(2)}) collective-permute-start(f32[48,512]{1,0:T(8,128)S(1)} %get-tuple-element.134), channel_id=1, source_target_pairs={{2,0},{3,1},{0,2},{1,3},{6,4},{7,5},{4,6},{5,7},{10,8},{11,9},{8,1... | collective-permute-start | bytes 294920 | tf_op jit(solution)/shard_map/ppermute | solution.py:47
  182.5 1.4 collective-permute-start.19
  183.9 2.8 %collective-permute-done.18.a_ref = f32[32,512]{1,0:T(8,128)S(1)} collective-permute-done((f32[32,512]{1,0:T(8,128)S(1)}, f32[32,512]{1,0:T(8,128)S(1)}, u32[]{:S(2)}, u32[]{:S(2)}) %collective-permute-start.18) | collective-permute-done | bytes 65568 | tf_op jit(solution)/shard_map/ppermute | solution.py:47
  186.7 1.2 collective-permute-done.19.b_ref
  188.5 1.5 collective-permute-start.20
  190.6 1.0 collective-permute-start.22
  191.6 0.9 collective-permute-done.20.one_ref
  192.5 2.6 %collective-permute-done.21.three_ref = f32[16,512]{1,0:T(8,128)S(1)} collective-permute-done((f32[16,512]{1,0:T(8,128)S(1)}, f32[16,512]{1,0:T(8,128)S(1)}, u32[]{:S(2)}, u32[]{:S(2)}) %collective-permute-start.21) | collective-permute-done | bytes 32800 | tf_op jit(solution)/shard_map/ppermute | solution.py:35
  195.1 0.9 collective-permute-done.22.two_ref
  196.0 1.2 z_place.1
  (70 shorter events, 5.9 us)
Async XLA Ops:
  7.2 134.9 %all-gather.2.cloned.1.call-start = ((), (), s32[]{:S(2)}) async-start(), calls=%async_computation.2 | async-start | bytes 4718592 | tf_op jit(solution)/shard_map/all_gather | solution.py:623
  7.2 14.2 %collective-permute-start = (bf16[256,1024]{1,0:T(8,128)(2,1)}, bf16[256,1024]{1,0:T(8,128)(2,1)S(1)}, u32[]{:S(2)}, u32[]{:S(2)}) collective-permute-start(bf16[256,1024]{1,0:T(8,128)(2,1)} %bitcast.30), channel_id=1, source_target_pairs={{16,0},{0,16},{48,32},{32,48},{80,64},{64,80},{112,96},{96,112},{1... | collective-permute-start | bytes 1572872 | tf_op jit(solution)/shard_map/ppermute | solution.py:35
  8.9 15.3 %collective-permute-start.1 = (bf16[256,1024]{1,0:T(8,128)(2,1)}, bf16[256,1024]{1,0:T(8,128)(2,1)S(1)}, u32[]{:S(2)}, u32[]{:S(2)}) collective-permute-start(bf16[256,1024]{1,0:T(8,128)(2,1)} %bitcast.31), channel_id=1, source_target_pairs={{32,0},{48,16},{64,32},{80,48},{96,64},{112,80},{0,96},{16,112},{3... | collective-permute-start | bytes 1572872 | tf_op jit(solution)/shard_map/ppermute | solution.py:35
  12.9 14.5 %collective-permute-start.2 = (bf16[256,1024]{1,0:T(8,128)(2,1)}, bf16[256,1024]{1,0:T(8,128)(2,1)S(1)}, u32[]{:S(2)}, u32[]{:S(2)}) collective-permute-start(bf16[256,1024]{1,0:T(8,128)(2,1)} %bitcast.32), channel_id=1, source_target_pairs={{96,0},{112,16},{0,32},{16,48},{32,64},{48,80},{64,96},{80,112},{9... | collective-permute-start | bytes 1572872 | tf_op jit(solution)/shard_map/ppermute | solution.py:35
  17.2 10.2 %copy-start.14 = (s32[1,256]{1,0:T(1,128)S(1)}, s32[1,256]{1,0:T(1,128)}, u32[]{:S(2)}) copy-start(s32[1,256]{1,0:T(1,128)} %param.6) | copy-start | bytes 3076
  21.5 15.8 %copy-start.7 = (bf16[256,1024]{1,0:T(8,128)(2,1)}, bf16[256,1024]{1,0:T(8,128)(2,1)S(1)}, u32[]{:S(2)}) copy-start(bf16[256,1024]{1,0:T(8,128)(2,1)S(1)} %collective-permute-done.refs_0_) | copy-start | bytes 1572868
  24.1 13.1 %copy-start.8 = (bf16[256,1024]{1,0:T(8,128)(2,1)}, bf16[256,1024]{1,0:T(8,128)(2,1)S(1)}, u32[]{:S(2)}) copy-start(bf16[256,1024]{1,0:T(8,128)(2,1)S(1)} %collective-permute-done.1.refs_1_) | copy-start | bytes 1572868
  27.4 6.5 %copy-start.9 = (bf16[256,1024]{1,0:T(8,128)(2,1)}, bf16[256,1024]{1,0:T(8,128)(2,1)S(1)}, u32[]{:S(2)}) copy-start(bf16[256,1024]{1,0:T(8,128)(2,1)S(1)} %collective-permute-done.2.refs_2_) | copy-start | bytes 1572868
  28.4 20.1 %all-to-all-start = ((bf16[8,272,128]{2,1,0:T(8,128)(2,1)}), bf16[8,272,128]{2,1,0:T(8,128)(2,1)S(1)}, u32[]{:S(2)}, u32[]{:S(2)}) async-start(bf16[8,272,128]{2,1,0:T(8,128)(2,1)} %pad_maximum_fusion.1), calls=%async_computation | async-start | bytes 1114112 | tf_op jit(solution)/shard_map/all_to_all | solution.py:633
  32.0 36.2 %collective-permute-start.3 = (bf16[256,1024]{1,0:T(8,128)(2,1)S(1)}, bf16[256,1024]{1,0:T(8,128)(2,1)S(1)}, u32[]{:S(2)}, u32[]{:S(2)}) collective-permute-start(bf16[256,1024]{1,0:T(8,128)(2,1)S(1)} %collective-permute-done.1.refs_1_), channel_id=1, source_target_pairs={{16,0},{0,16},{48,32},{32,48},{80,64},{64,80},{112,96},{96,112},{1... | collective-permute-start | bytes 1572872 | tf_op jit(solution)/shard_map/ppermute | solution.py:35
  33.9 34.3 %collective-permute-start.4 = (bf16[256,1024]{1,0:T(8,128)(2,1)S(1)}, bf16[256,1024]{1,0:T(8,128)(2,1)S(1)}, u32[]{:S(2)}, u32[]{:S(2)}) collective-permute-start(bf16[256,1024]{1,0:T(8,128)(2,1)S(1)} %collective-permute-done.1.refs_1_), channel_id=1, source_target_pairs={{32,0},{48,16},{64,32},{80,48},{96,64},{112,80},{0,96},{16,112},{3... | collective-permute-start | bytes 1572872 | tf_op jit(solution)/shard_map/ppermute | solution.py:35
  36.6 31.5 %collective-permute-start.5 = (bf16[256,1024]{1,0:T(8,128)(2,1)S(1)}, bf16[256,1024]{1,0:T(8,128)(2,1)S(1)}, u32[]{:S(2)}, u32[]{:S(2)}) collective-permute-start(bf16[256,1024]{1,0:T(8,128)(2,1)S(1)} %collective-permute-done.refs_0_), channel_id=1, source_target_pairs={{96,0},{112,16},{0,32},{16,48},{32,64},{48,80},{64,96},{80,112},{9... | collective-permute-start | bytes 1572872 | tf_op jit(solution)/shard_map/ppermute | solution.py:35
  48.5 32.5 %copy-start.6 = (bf16[8,272,128]{2,1,0:T(8,128)(2,1)}, bf16[8,272,128]{2,1,0:T(8,128)(2,1)S(1)}, u32[]{:S(2)}) copy-start(bf16[8,272,128]{2,1,0:T(8,128)(2,1)S(1)} %all-to-all-done.head_ref) | copy-start | bytes 1671172
  68.1 6.6 %copy-start.4 = (bf16[256,1024]{1,0:T(8,128)(2,1)}, bf16[256,1024]{1,0:T(8,128)(2,1)S(1)}, u32[]{:S(2)}) copy-start(bf16[256,1024]{1,0:T(8,128)(2,1)S(1)} %collective-permute-done.3.refs_0_) | copy-start | bytes 1572868
  68.1 6.6 %copy-start.3 = (bf16[256,1024]{1,0:T(8,128)(2,1)}, bf16[256,1024]{1,0:T(8,128)(2,1)S(1)}, u32[]{:S(2)}) copy-start(bf16[256,1024]{1,0:T(8,128)(2,1)S(1)} %collective-permute-done.4.refs_1_) | copy-start | bytes 1572868
  68.1 6.6 %copy-start.5 = (bf16[256,1024]{1,0:T(8,128)(2,1)}, bf16[256,1024]{1,0:T(8,128)(2,1)S(1)}, u32[]{:S(2)}) copy-start(bf16[256,1024]{1,0:T(8,128)(2,1)S(1)} %collective-permute-done.5.refs_2_) | copy-start | bytes 1572868
  68.2 12.9 %collective-permute-start.6 = (bf16[96,1024]{1,0:T(8,128)(2,1)S(1)}, bf16[96,1024]{1,0:T(8,128)(2,1)S(1)}, u32[]{:S(2)}, u32[]{:S(2)}) collective-permute-start(bf16[96,1024]{1,0:T(8,128)(2,1)S(1)} %slice.18), channel_id=1, source_target_pairs={{16,0},{0,16},{48,32},{32,48},{80,64},{64,80},{112,96},{96,112},{1... | collective-permute-start | bytes 589832 | tf_op jit(solution)/shard_map/ppermute | solution.py:35
  69.2 11.8 %collective-permute-start.7 = (bf16[80,1024]{1,0:T(8,128)(2,1)S(1)}, bf16[80,1024]{1,0:T(8,128)(2,1)S(1)}, u32[]{:S(2)}, u32[]{:S(2)}) collective-permute-start(bf16[80,1024]{1,0:T(8,128)(2,1)S(1)} %slice.19), channel_id=1, source_target_pairs={{32,0},{48,16},{64,32},{80,48},{96,64},{112,80},{0,96},{16,112},{3... | collective-permute-start | bytes 491528 | tf_op jit(solution)/shard_map/ppermute | solution.py:35
  72.0 9.0 %collective-permute-start.8 = (bf16[80,1024]{1,0:T(8,128)(2,1)S(1)}, bf16[80,1024]{1,0:T(8,128)(2,1)S(1)}, u32[]{:S(2)}, u32[]{:S(2)}) collective-permute-start(bf16[80,1024]{1,0:T(8,128)(2,1)S(1)} %slice.20), channel_id=1, source_target_pairs={{96,0},{112,16},{0,32},{16,48},{32,64},{48,80},{64,96},{80,112},{9... | collective-permute-start | bytes 491528 | tf_op jit(solution)/shard_map/ppermute | solution.py:35
  91.8 4.8 %collective-permute-start.9 = (f32[4,2048]{1,0:T(4,128)}, f32[4,2048]{1,0:T(4,128)S(1)}, u32[]{:S(2)}, u32[]{:S(2)}) collective-permute-start(f32[4,2048]{1,0:T(4,128)} %get-tuple-element.103), channel_id=1, source_target_pairs={{16,0},{0,16},{48,32},{32,48},{80,64},{64,80},{112,96},{96,112},{1... | collective-permute-start | bytes 98312 | tf_op jit(solution)/shard_map/ppermute | solution.py:35
  97.4 10.9 %copy-start.10 = (f32[2,4,2048]{2,1,0:T(4,128)}, f32[2,4,2048]{2,1,0:T(4,128)S(1)}, u32[]{:S(2)}) copy-start(f32[2,4,2048]{2,1,0:T(4,128)S(1)} %pad_maximum_fusion.3.own_ref) | copy-start | bytes 196612
  97.4 5.2 %collective-permute-start.10 = (f32[2,4,2048]{2,1,0:T(4,128)S(1)}, f32[2,4,2048]{2,1,0:T(4,128)S(1)}, u32[]{:S(2)}, u32[]{:S(2)}) collective-permute-start(f32[2,4,2048]{2,1,0:T(4,128)S(1)} %pad_maximum_fusion.3.own_ref), channel_id=1, source_target_pairs={{32,0},{48,16},{64,32},{80,48},{96,64},{112,80},{0,96},{16,112},{3... | collective-permute-start | bytes 196616 | tf_op jit(solution)/shard_map/ppermute | solution.py:35
  100.7 7.6 %collective-permute-start.11 = (f32[2,4,2048]{2,1,0:T(4,128)S(1)}, f32[2,4,2048]{2,1,0:T(4,128)S(1)}, u32[]{:S(2)}, u32[]{:S(2)}) collective-permute-start(f32[2,4,2048]{2,1,0:T(4,128)S(1)} %pad_maximum_fusion.3.own_ref), channel_id=1, source_target_pairs={{96,0},{112,16},{0,32},{16,48},{32,64},{48,80},{64,96},{80,112},{9... | collective-permute-start | bytes 196616 | tf_op jit(solution)/shard_map/ppermute | solution.py:35
  100.7 7.6 %collective-permute-start.12 = (f32[2,4,2048]{2,1,0:T(4,128)S(1)}, f32[2,4,2048]{2,1,0:T(4,128)S(1)}, u32[]{:S(2)}, u32[]{:S(2)}) collective-permute-start(f32[2,4,2048]{2,1,0:T(4,128)S(1)} %pad_maximum_fusion.3.own_ref), channel_id=1, source_target_pairs={{64,0},{80,16},{96,32},{112,48},{0,64},{16,80},{32,96},{48,112},{6... | collective-permute-start | bytes 196616 | tf_op jit(solution)/shard_map/ppermute | solution.py:35
  102.6 5.7 %copy-start.11 = (f32[2,4,2048]{2,1,0:T(4,128)}, f32[2,4,2048]{2,1,0:T(4,128)S(1)}, u32[]{:S(2)}) copy-start(f32[2,4,2048]{2,1,0:T(4,128)S(1)} %collective-permute-done.10.one_ref) | copy-start | bytes 196612
  108.3 0.6 copy-start.12
  108.3 0.7 copy-start.13
  131.2 33.2 %all-to-all-start.1 = ((bf16[8,256,640]{2,1,0:T(8,128)(2,1)}), bf16[8,256,640]{2,1,0:T(8,128)(2,1)S(1)}, u32[]{:S(2)}, u32[]{:S(2)}) async-start(bf16[8,256,640]{2,1,0:T(8,128)(2,1)} %attention_backward.1.grad_ref.gated_ref), calls=%async_computation.1 | async-start | bytes 5242880 | tf_op jit(solution)/shard_map/all_to_all | solution.py:650
  145.6 3.4 %collective-permute-start.13 = (f32[8,80,512]{2,1,0:T(8,128)}, f32[8,80,512]{2,1,0:T(8,128)}, u32[]{:S(2)}, u32[]{:S(2)}) collective-permute-start(f32[8,80,512]{2,1,0:T(8,128)} %get-tuple-element.116), channel_id=1, source_target_pairs={{1,0},{0,1},{3,2},{2,3},{5,4},{4,5},{7,6},{6,7},{9,8},{8,9},{11,10... | collective-permute-start | bytes 3932168 | tf_op jit(solution)/shard_map/ppermute | solution.py:39
  164.4 4.9 %copy-start.2 = (bf16[8,256,640]{2,1,0:T(8,128)(2,1)}, bf16[8,256,640]{2,1,0:T(8,128)(2,1)S(1)}, u32[]{:S(2)}) copy-start(bf16[8,256,640]{2,1,0:T(8,128)(2,1)S(1)} %all-to-all-done.1.gated_ref.grad_ref) | copy-start | bytes 7864324
  164.4 14.5 %copy-start = (f32[2,80,512]{2,1,0:T(8,128)S(1)}, f32[2,80,512]{2,1,0:T(8,128)}, u32[]{:S(2)}) copy-start(f32[2,80,512]{2,1,0:T(8,128)} %get-tuple-element.129.own_ref) | copy-start | bytes 983044
  164.4 14.6 %copy-start.1 = (s32[4]{0:T(128)S(1)}, s32[4]{0:T(128)}, u32[]{:S(2)}) copy-start(s32[4]{0:T(128)} %pad_add_fusion.3.pos_ref) | copy-start | bytes 52
  164.5 14.5 %collective-permute-start.14 = (bf16[2,80,512]{2,1,0:T(8,128)(2,1)}, bf16[2,80,512]{2,1,0:T(8,128)(2,1)S(1)}, u32[]{:S(2)}, u32[]{:S(2)}) collective-permute-start(bf16[2,80,512]{2,1,0:T(8,128)(2,1)} %get-tuple-element.121), channel_id=1, source_target_pairs={{4,0},{5,1},{6,2},{7,3},{8,4},{9,5},{10,6},{11,7},{12,8},{13,9},{1... | collective-permute-start | bytes 491528 | tf_op jit(solution)/shard_map/ppermute | solution.py:39
  167.1 11.9 %collective-permute-start.15 = (bf16[2,80,512]{2,1,0:T(8,128)(2,1)}, bf16[2,80,512]{2,1,0:T(8,128)(2,1)S(1)}, u32[]{:S(2)}, u32[]{:S(2)}) collective-permute-start(bf16[2,80,512]{2,1,0:T(8,128)(2,1)} %get-tuple-element.122), channel_id=1, source_target_pairs={{12,0},{13,1},{14,2},{15,3},{0,4},{1,5},{2,6},{3,7},{4,8},{5,9},{6... | collective-permute-start | bytes 491528 | tf_op jit(solution)/shard_map/ppermute | solution.py:39
  167.1 11.9 %collective-permute-start.16 = (bf16[2,80,512]{2,1,0:T(8,128)(2,1)}, bf16[2,80,512]{2,1,0:T(8,128)(2,1)S(1)}, u32[]{:S(2)}, u32[]{:S(2)}) collective-permute-start(bf16[2,80,512]{2,1,0:T(8,128)(2,1)} %get-tuple-element.123), channel_id=1, source_target_pairs={{8,0},{9,1},{10,2},{11,3},{12,4},{13,5},{14,6},{15,7},{0,8},{1,9},... | collective-permute-start | bytes 491528 | tf_op jit(solution)/shard_map/ppermute | solution.py:39
  179.7 8.2 %collective-permute-start.17 = (f32[48,512]{1,0:T(8,128)S(1)}, f32[48,512]{1,0:T(8,128)S(1)}, u32[]{:S(2)}, u32[]{:S(2)}) collective-permute-start(f32[48,512]{1,0:T(8,128)S(1)} %get-tuple-element.134), channel_id=1, source_target_pairs={{2,0},{3,1},{0,2},{1,3},{6,4},{7,5},{4,6},{5,7},{10,8},{11,9},{8,1... | collective-permute-start | bytes 294920 | tf_op jit(solution)/shard_map/ppermute | solution.py:47
  182.4 4.3 %collective-permute-start.18 = (f32[32,512]{1,0:T(8,128)S(1)}, f32[32,512]{1,0:T(8,128)S(1)}, u32[]{:S(2)}, u32[]{:S(2)}) collective-permute-start(f32[32,512]{1,0:T(8,128)S(1)} %get-tuple-element.135), channel_id=1, source_target_pairs={{16,0},{17,1},{18,2},{19,3},{20,4},{21,5},{22,6},{23,7},{24,8},{25... | collective-permute-start | bytes 196616 | tf_op jit(solution)/shard_map/ppermute | solution.py:47
  182.5 5.5 %collective-permute-start.19 = (f32[32,512]{1,0:T(8,128)S(1)}, f32[32,512]{1,0:T(8,128)S(1)}, u32[]{:S(2)}, u32[]{:S(2)}) collective-permute-start(f32[32,512]{1,0:T(8,128)S(1)} %get-tuple-element.136), channel_id=1, source_target_pairs={{18,0},{19,1},{16,2},{17,3},{22,4},{23,5},{20,6},{21,7},{26,8},{27... | collective-permute-start | bytes 196616 | tf_op jit(solution)/shard_map/ppermute | solution.py:47
  188.5 4.0 %collective-permute-start.20 = (f32[16,512]{1,0:T(8,128)S(1)}, f32[16,512]{1,0:T(8,128)S(1)}, u32[]{:S(2)}, u32[]{:S(2)}) collective-permute-start(f32[16,512]{1,0:T(8,128)S(1)} %get-tuple-element.138), channel_id=1, source_target_pairs={{32,0},{48,16},{64,32},{80,48},{96,64},{112,80},{0,96},{16,112},{3... | collective-permute-start | bytes 98312 | tf_op jit(solution)/shard_map/ppermute | solution.py:35
  190.0 5.1 %collective-permute-start.21 = (f32[16,512]{1,0:T(8,128)S(1)}, f32[16,512]{1,0:T(8,128)S(1)}, u32[]{:S(2)}, u32[]{:S(2)}) collective-permute-start(f32[16,512]{1,0:T(8,128)S(1)} %get-tuple-element.139), channel_id=1, source_target_pairs={{96,0},{112,16},{0,32},{16,48},{32,64},{48,80},{64,96},{80,112},{9... | collective-permute-start | bytes 98312 | tf_op jit(solution)/shard_map/ppermute | solution.py:35
  190.6 5.4 %collective-permute-start.22 = (f32[16,512]{1,0:T(8,128)S(1)}, f32[16,512]{1,0:T(8,128)S(1)}, u32[]{:S(2)}, u32[]{:S(2)}) collective-permute-start(f32[16,512]{1,0:T(8,128)S(1)} %get-tuple-element.140), channel_id=1, source_target_pairs={{64,0},{80,16},{96,32},{112,48},{0,64},{16,80},{32,96},{48,112},{6... | collective-permute-start | bytes 98312 | tf_op jit(solution)/shard_map/ppermute | solution.py:35
Sparse Core Ops, SparseCore 0:
  27.6 111.7 all-gather.1
where the time goes:
time: 205 us; the launch traced here: 204 us
  Pallas kernels  72.9 us (36%)
  waiting for transfers between devices  64.1 us (31%)
  starting transfers between devices  39.7 us (19%)
  between operations  14.3 us (7%)
  other arithmetic  8.15 us (4%)
  local copies, waits for them, and re-layouts  2.53 us (1%)
  matrix products  2.51 us (1%)
    ppermute x16, waiting for transfers between devices, from_seq(): return lax.ppermute(a, 'seq', seq_perm(dz, dx))  39.5 us
    ppermute x16, starting transfers between devices, from_seq(): return lax.ppermute(a, 'seq', seq_perm(dz, dx))  22.8 us
    pallas_call x4, Pallas kernels, ln_proj(): pl.pallas_call(functools.partial(ln_proj_kernel, len(blocks)), grid_spec=...  18.8 us
    pallas_call x1, Pallas kernels, backward(): pl.pallas_call(backward_kernel, in_specs=[vmem()] * 5 + [pl.BlockSpec(mem...  15.3 us
    all_to_all x1, waiting for transfers between devices, local(): back_tok = lax.all_to_all(back, 'seq', 0, 0, tiled=True)  12.7 us
    pallas_call x1, Pallas kernels, shard_outputs(): pl.pallas_call(shard_kernel, grid=(4,), in_specs=[pl.BlockSpec((H, rows,...  9.62 us
    pallas_call x1, Pallas kernels, mix(): pl.pallas_call(mix_kernel, grid=(length // tile,), in_specs=[pl.BlockSpec...  7.05 us
    pallas_call x1, Pallas kernels, forward(): pl.pallas_call(forward_kernel, in_specs=[vmem()] * 3, out_specs=[vmem()]...  6.82 us
  transfers between devices with their start and end apart: 26, of which 14 were waited for; matrix products, arithmetic and copies ran while one was open for 6% of the time, Pallas kernels for 34%

commit v1 on v0

--- a/solution.py
+++ b/solution.py
@@ -263,57 +263,46 @@
 
 
 def mix_kernel(own_ref, one_ref, three_ref, two_ref, att_ref, gate_ref, gg_ref, slope_ref, early_ref, go_ref, got_ref):
+    length = att_ref.shape[1]
     width = H * HD
+    tile = 2 * HD
     heads = [ref[k] for ref in (own_ref, one_ref, three_ref, two_ref) for k in range(NX)]
     mean_all = sum(a[0:1] for a in heads) * (1.0 / H)
     apart = [a[0:1] - mean_all for a in heads]
     spread = sum(a[1:2] for a in heads) + HD * sum(d * d for d in apart)
-    inverse = lax.rsqrt(spread * (1.0 / width) + EPS)
-    first = sum(a[2:3] for a in heads) * (1.0 / width)
-    second = inverse * sum(a[3:4] + d * a[2:3] for a, d in zip(heads, apart)) * (1.0 / width)
-    gate = gate_ref[...].astype(F32)
-    gg = gg_ref[...].astype(F32)
-    mixed = (att_ref[...] - mean_all) * inverse
-    grad_att = inverse * (gg * gate - first - mixed * second)
-    got_ref[...] = grad_att.astype(BF16)
-    go_ref[...] = grad_att.T.astype(BF16)
-    gated = (mixed * gate).astype(BF16).T
-    grad_u = (gg * mixed).T
-    late = pl.program_id(0) >= NZ * NX // 2
-
-    def put(order):
+    inverse_all = lax.rsqrt(spread * (1.0 / width) + EPS)
+    first_all = sum(a[2:3] for a in heads) * (1.0 / width)
+    second_all = inverse_all * sum(a[3:4] + d * a[2:3] for a, d in zip(heads, apart)) * (1.0 / width)
+    for i in range(0, length, tile):
+        at = slice(i, i + tile)
+        gate = gate_ref[:, at].astype(F32)
+        gg = gg_ref[:, at].astype(F32)
+        inverse = inverse_all[:, at]
+        mixed = (att_ref[:, at] - mean_all[:, at]) * inverse
+        grad_att = inverse * (gg * gate - first_all[:, at] - mixed * second_all[:, at])
+        got_ref[:, at] = grad_att.astype(BF16)
+        go_ref[at, :] = grad_att.T.astype(BF16)
+        gated = (mixed * gate).astype(BF16).T
+        grad_u = ((gg * mixed).T * time_rows(slope_ref, i, tile, 0)).astype(BF16)
         for k in range(2):
-            at = slice(k * HD, (k + 1) * HD)
-            early_ref[order[k], 0, :, :HD] = gated[at]
-            early_ref[order[k], 0, :, HD:] = (grad_u[at] * slope_ref[0, order[k]]).astype(BF16)
-
-    pl.when(jnp.logical_not(late))(lambda: put((0, 1)))
-    pl.when(late)(lambda: put((1, 0)))
+            shard, row = tile_place(i // HD + k)
+            early_ref[shard, row : row + HD, :HD] = gated[k * HD : (k + 1) * HD]
+            early_ref[shard, row : row + HD, HD:] = grad_u[k * HD : (k + 1) * HD]
 
 
 def mix(own, one, three, two, att, gate, gg, slope):
     length = att.shape[1]
     shards = NZ * NX
-    tile = 2 * HD
-    turn = shards // 2
-
-    def pair(i):
-        return jnp.where(i < turn, i, 2 * turn - 1 - i)
-
-    by_tile = pl.BlockSpec((HD, tile), lambda i: (0, i))
+    whole = lambda shape: pl.BlockSpec(shape, lambda i: (0,) * len(shape))
     return pl.pallas_call(
         mix_kernel,
-        grid=(length // tile,),
-        in_specs=[pl.BlockSpec((NX, 4, tile), lambda i: (0, 0, i))] * 4
-        + [by_tile] * 3
-        + [pl.BlockSpec((1, 2, HD, HD), lambda i: (i // turn, pair(i), 0, 0))],
-        out_specs=[
-            pl.BlockSpec((2, 1, HD, tile), lambda i: (pair(i), i // turn, 0, 0)),
-            pl.BlockSpec((tile, HD), lambda i: (i, 0)),
-            by_tile,
-        ],
+        grid=(1,),
+        in_specs=[whole(own.shape)] * 4
+        + [whole(att.shape)] * 3
+        + [pl.BlockSpec(slope.shape[:3] + (HD,), lambda i: (0, 0, 0, 0))],
+        out_specs=[whole((shards, length // shards, 2 * HD)), whole((length, HD)), whole((HD, length))],
         out_shape=(
-            jax.ShapeDtypeStruct((shards, 2, HD, tile), BF16),
+            jax.ShapeDtypeStruct((shards, length // shards, 2 * HD), BF16),
             jax.ShapeDtypeStruct((length, HD), BF16),
             jax.ShapeDtypeStruct((HD, length), BF16),
         ),
@@ -327,11 +316,8 @@
     length = go_ref.shape[0]
     copy = pltpu.make_async_copy(slope_hbm, slope_ref, sem)
     copy.start()
-    for shard in range(NZ * NX):
-        for k in range(2):
-            rows = slice(k * HD, (k + 1) * HD)
-            back_ref[shard, rows, :HD] = early_ref[shard, k, :, HD:]
-            back_ref[shard, rows, 4 * HD :] = early_ref[shard, k, :, :HD]
+    back_ref[:, :, :HD] = early_ref[:, :, HD:]
+    back_ref[:, :, 4 * HD :] = early_ref[:, :, :HD]
     keys = [time_rows(act_ref, j, BK, 3) for j in range(0, length, BK)]
     keys_t = [k.T for k in keys]
     values = [time_rows(act_ref, j, BK, 1) for j in range(0, length, BK)]
@@ -543,54 +529,83 @@
     w_out_ref[:, 4 * HD :] = out_ref[8:] * factor
 
 
-def shard_kernel(gated_ref, grad_ref, w_in_ref, w_out_ref, hist_ref, cot_ref, layer_ref, grad_hist_ref, acc_ref):
-    step = pl.program_id(0)
-
-    def columns(ref):
-        return jnp.concatenate([ref[h] for h in range(H)], axis=1)
-
+def columns(ref):
+    return jnp.concatenate([ref[h] for h in range(H)], axis=1)
+
+
+def shard_out_kernel(gated_ref, grad_ref, w_in_ref, w_out_ref, hist_ref, layer_ref, acc_ref):
     term = dot_nt(columns(grad_ref), w_in_ref[...])
 
-    @pl.when(step == 0)
+    @pl.when(pl.program_id(0) == 0)
     def _():
         hist = hist_ref[...].astype(F32)
         layer_ref[...] = (hist + dot(columns(gated_ref), w_out_ref[...])).astype(BF16)
         acc_ref[...] = term
 
-    @pl.when(step > 0)
+    @pl.when(pl.program_id(0) > 0)
     def _():
         acc_ref[...] += term
 
-    @pl.when(step == 3)
+
+def shard_grad_kernel(grad_ref, w_in_ref, hist_ref, cot_ref, half_ref, grad_hist_ref, acc_ref):
+    term = dot_nt(columns(grad_ref), w_in_ref[...])
+
+    @pl.when(pl.program_id(0) == 0)
+    def _():
+        acc_ref[...] = half_ref[...] + term
+
+    @pl.when(pl.program_id(0) > 0)
     def _():
         normed, inverse = layer_norm(hist_ref[...].astype(F32))
-        grad = norm_back(normed, inverse, acc_ref[...])
+        grad = norm_back(normed, inverse, acc_ref[...] + term)
         grad_hist_ref[...] = (cot_ref[...].astype(F32) + grad).astype(BF16)
 
 
-def shard_outputs(back, w_in, w_out, hist, cot):
+def shard_out(back, w_in, w_out, hist):
     rows, width = hist.shape
     whole = lambda a: pl.BlockSpec(a.shape, lambda k: (0,) * a.ndim)
     return pl.pallas_call(
-        shard_kernel,
-        grid=(4,),
+        shard_out_kernel,
+        grid=(2,),
         in_specs=[
             pl.BlockSpec((H, rows, HD), lambda k: (0, 0, 4)),
             pl.BlockSpec((H, rows, HD), lambda k: (0, 0, k)),
             pl.BlockSpec((width, width), lambda k: (0, k)),
             whole(w_out),
             whole(hist),
-            whole(cot),
         ],
         out_specs=[whole(hist)] * 2,
-        out_shape=[jax.ShapeDtypeStruct(hist.shape, BF16)] * 2,
+        out_shape=[jax.ShapeDtypeStruct(hist.shape, BF16), jax.ShapeDtypeStruct(hist.shape, F32)],
+        compiler_params=params(LIMIT),
+        cost_estimate=pl.CostEstimate(
+            flops=6 * rows * width * width, bytes_accessed=8 << 20, transcendentals=0
+        ),
+        name="shard_out",
+    )(back, back, w_in, w_out, hist)
+
+
+def shard_grad(back, w_in, hist, cot, half):
+    rows, width = hist.shape
+    whole = lambda a: pl.BlockSpec(a.shape, lambda k: (0,) * a.ndim)
+    return pl.pallas_call(
+        shard_grad_kernel,
+        grid=(2,),
+        in_specs=[
+            pl.BlockSpec((H, rows, HD), lambda k: (0, 0, 2 + k)),
+            pl.BlockSpec((width, width), lambda k: (0, 2 + k)),
+            whole(hist),
+            whole(cot),
+            whole(half),
+        ],
+        out_specs=whole(hist),
+        out_shape=jax.ShapeDtypeStruct(hist.shape, BF16),
         scratch_shapes=[pltpu.VMEM((rows, width), F32)],
         compiler_params=params(LIMIT),
         cost_estimate=pl.CostEstimate(
-            flops=10 * rows * width * width, bytes_accessed=14 << 20, transcendentals=0
-        ),
-        name="shard_outputs",
-    )(back, back, w_in, w_out, hist, cot)
+            flops=4 * rows * width * width, bytes_accessed=8 << 20, transcendentals=0
+        ),
+        name="shard_grad",
+    )(back, w_in, hist, cot, half)
 
 
 def local(history, segment_ids, w_in, w_out, cotangent):
@@ -619,8 +634,6 @@
     got = step_one(hist)
     outs = project({(0, 0): hist}, ())
     grad_gated_own = dot_nt(cot, w_out).astype(BF16).reshape(rows, H, HD).transpose(1, 0, 2)
-    got, outs, grad_gated_own, cot_next = tie((got, outs, grad_gated_own, cot))
-    cot_all = lax.all_gather(cot_next, "seq", axis=0, tiled=True)
     ids = segment_ids[0].astype(BF16).reshape(2, HD)
     ids = jnp.pad(ids, ((0, 14), (0, 0)))
     to_heads = jnp.concatenate(
@@ -631,22 +644,26 @@
         axis=1,
     )
     at_head = lax.all_to_all(to_heads, "seq", 0, 0, tiled=True)
+    cot_wide = jnp.broadcast_to(cot[None], (NZ * NX, rows, width))
+    got, outs, cot_wide = tie((got, outs, cot_wide))
     more = step_two(got)
     outs = project(got, outs)
-    more, outs = tie((more, outs))
+    more, outs, cot_wide = tie((more, outs, cot_wide))
     got.update(more)
     last = step_three(got)
     outs = project(more, outs)
     ids = at_head[:, rows : rows + 2].astype(jnp.int32)
     ids = jnp.concatenate([ids[:, 0], ids[::-1, 1]], axis=0).reshape(1, length)
     start = sum(jnp.where(ids > v, jnp.sum((ids == v).astype(jnp.int32)), 0) for v in range(3))
-    last, outs, start, at_head = tie((last, outs, start, at_head))
+    last, outs, start, at_head, cot_wide = tie((last, outs, start, at_head, cot_wide))
+    cot_all = lax.all_to_all(cot_wide, "seq", 0, 0, tiled=True).reshape(length, width)
     normed_t, act, slope = project(last, outs)
     att, gate_t, gg_t, stats = forward(act, at_head, start)
     pair = jnp.stack([stats, from_seq(stats, 0, 1)])
     others = [from_seq(pair, dz, 0) for dz in (1, 3, 2)]
     early, grad_out, grad_out_t = mix(pair, *others, att, gate_t, gg_t, slope)
     back = backward(act, grad_out, grad_out_t, start, early, slope)
+    back, cot_all = tie((back, cot_all))
     back_tok = lax.all_to_all(back, "seq", 0, 0, tiled=True)
 
     at_core = core.reshape(1)
@@ -663,10 +680,10 @@
         [((NXH, 80, n), F32)] + [((NXH, 80, n), BF16)] * 3,
         limit=LIMIT,
     )
-    back_tok, own, sends = tie((back_tok, own, sends))
+    own, sends = tie((own, sends))
     sends = [from_user(a, d, 0, 0) for a, d in zip(sends, (1, 3, 2))]
-    layer_out, grad_history = shard_outputs(back_tok, w_in, w_out, hist, cot)
-    sends, layer_out, grad_history = tie((sends, layer_out, grad_history))
+    layer_out, half = shard_out(back_tok, w_in, w_out, hist)
+    sends, layer_out, half = tie((sends, layer_out, half))
     keep, same, one, two = small(
         y_sum_kernel,
         "y_sum",
@@ -678,6 +695,8 @@
     same = from_both(same, 1, 0)
     one = from_both(one, 0, 1)
     two = from_both(two, 1, 1)
+    grad_history = shard_grad(back_tok, w_in, hist, cot, half)
+    same, one, two, grad_history = tie((same, one, two, grad_history))
     own, *sends, own_out = small(
         x_sum_kernel,
         "x_sum",

time: 205 us -> 189 us (0.922)
  between operations: 14.3 us -> 0.87 us
  waiting for transfers between devices: 64.1 us -> 54.2 us
  starting transfers between devices: 39.7 us -> 44 us
  local copies, waits for them, and re-layouts: 2.53 us -> 6.52 us
    all_to_all x1, waiting for transfers between devices: 12.7 us -> 4.71 us  [local(): back_tok = lax.all_to_all(back, 'seq', 0, 0, tiled=True)]
    ppermute x16, waiting for transfers between devices: 39.5 us -> 46.7 us  [from_seq(): return lax.ppermute(a, 'seq', seq_perm(dz, dx))]
    all_to_all x1, waiting for transfers between devices: 5.05 us -> 0.01 us  [local(): at_head = lax.all_to_all(to_heads, 'seq', 0, 0, tiled=True)]
    all_to_all x0 -> x1, starting transfers between devices: none -> 4.74 us  [local(): lax.all_to_all(cot_wide, 'seq', 0, 0, tiled=True).reshape(length, width)]
    ppermute x3, waiting for transfers between devices: 4.06 us -> 0.01 us  [from_both(): return lax.ppermute(a, ('seq', 'user'), pairs)]
    broadcast_in_dim x0 -> x1, local copies, waits for them, and re-layouts: none -> 2.49 us  [local(): cot_wide = jnp.broadcast_to(cot[None], (NZ * NX, rows, width))]
    pallas_call x2 -> x3, Pallas kernels: 16.7 us -> 15.9 us  [the longest x1 6.19 us: shard_out(): pl.pallas_call(shard_out_kernel, grid=(2,), in_specs=[pl.BlockSpec((H, ro...]
  transfers between devices with their start and end apart: 26 -> 26, of which waited for: 14 -> 11; matrix products, arithmetic and copies ran while one was open for 6% -> 7% of each run, Pallas kernels for 34% -> 37%
where the time goes in v1:
time: 189 us; the launch traced here: 188 us
  Pallas kernels  72.1 us (38%)
  waiting for transfers between devices  54.2 us (29%)
  starting transfers between devices  44 us (23%)
  other arithmetic  8.04 us (4%)
  local copies, waits for them, and re-layouts  6.52 us (3%)
  matrix products  2.51 us (1%)
    ppermute x16, waiting for transfers between devices, from_seq(): return lax.ppermute(a, 'seq', seq_perm(dz, dx))  46.7 us
    ppermute x16, starting transfers between devices, from_seq(): return lax.ppermute(a, 'seq', seq_perm(dz, dx))  21.1 us
    pallas_call x4, Pallas kernels, ln_proj(): pl.pallas_call(functools.partial(ln_proj_kernel, len(blocks)), grid_spec=...  18.9 us
    pallas_call x1, Pallas kernels, backward(): pl.pallas_call(backward_kernel, in_specs=[vmem()] * 5 + [pl.BlockSpec(mem...  15.2 us
    pallas_call x1, Pallas kernels, forward(): pl.pallas_call(forward_kernel, in_specs=[vmem()] * 3, out_specs=[vmem()]...  6.83 us
    pallas_call x1, Pallas kernels, terms_in(): pl.pallas_call(terms_in_kernel, grid=(4,), in_specs=[smem(), pl.BlockSpec...  6.54 us
    pallas_call x1, Pallas kernels, shard_out(): pl.pallas_call(shard_out_kernel, grid=(2,), in_specs=[pl.BlockSpec((H, ro...  6.19 us
    pallas_call x1, Pallas kernels, shard_grad(): pl.pallas_call(shard_grad_kernel, grid=(2,), in_specs=[pl.BlockSpec((H, r...  5.47 us
  transfers between devices with their start and end apart: 26, of which 11 were waited for; matrix products, arithmetic and copies ran while one was open for 7% of the time, Pallas kernels for 37%

profile of v1, /device:TPU:0, one launch (start us, length us, event | category | flops | bytes accessed | tf_op | source)
XLA Modules:
  0.0 188.2 jit_solution(8390712846964162631)
XLA Ops:
  0.6 1.7 collective-permute-start
  2.3 4.0 %collective-permute-start.1 = (bf16[256,1024]{1,0:T(8,128)(2,1)}, bf16[256,1024]{1,0:T(8,128)(2,1)S(1)}, u32[]{:S(2)}, u32[]{:S(2)}) collective-permute-start(bf16[256,1024]{1,0:T(8,128)(2,1)} %bitcast.32), channel_id=1, source_target_pairs={{32,0},{48,16},{64,32},{80,48},{96,64},{112,80},{0,96},{16,112},{3... | collective-permute-start | bytes 1572872 | tf_op jit(solution)/shard_map/ppermute | solution.py:35
  6.3 2.5 %convolution_convert_fusion = bf16[256,1024]{1,0:T(8,128)(2,1)S(1)} fusion(bf16[1024,1024]{1,0:T(8,128)(2,1)} %w_out_ref.1, bf16[1,256,1024]{2,1,0:T(8,128)(2,1)} %param.9), kind=kOutput, calls=%fused_computation | convolution fusion | flops 537133056 | bytes 3145728 | tf_op jit(solution)/shard_map/dot_general | solution.py:97
  9.4 0.9 pad_maximum_fusion.1
  10.2 4.5 %all-to-all-start = ((bf16[8,272,128]{2,1,0:T(8,128)(2,1)}), bf16[8,272,128]{2,1,0:T(8,128)(2,1)S(1)}, u32[]{:S(2)}, u32[]{:S(2)}) async-start(bf16[8,272,128]{2,1,0:T(8,128)(2,1)} %pad_maximum_fusion.1), calls=%async_computation | async-start | bytes 1114112 | tf_op jit(solution)/shard_map/all_to_all | solution.py:646
  14.8 1.3 constant_dynamic-slice_fusion.3
  16.1 1.1 pad_maximum_fusion.refs_1_.refs_3_
  17.2 3.1 %ln_proj.4 = (bf16[1024,2048]{1,0:T(8,128)(2,1)}, bf16[2,8,128,512]{3,2,1,0:T(8,128)(2,1)}, f32[2,8,128,512]{3,2,1,0:T(8,128)}) custom-call(s32[1]{0:T(128)} %bitcast.7.at_ref, bf16[256,1024]{1,0:T(8,128)(2,1)} %bitcast.34, bf16[1024,512]{1,0:T(8,128)(2,1)} %pad_maximum_fusion.refs_1_.refs_3_), custom_call_target="tpu_custom_call" | custom-call | flops 268435456 | bytes 3145728 | tf_op jit(solution)/shard_map/ln_proj/pallas_call | solution.py:144
  20.3 2.5 %collective-permute-done.1.refs_1_ = bf16[256,1024]{1,0:T(8,128)(2,1)S(1)} collective-permute-done((bf16[256,1024]{1,0:T(8,128)(2,1)}, bf16[256,1024]{1,0:T(8,128)(2,1)S(1)}, u32[]{:S(2)}, u32[]{:S(2)}) %collective-permute-start.1) | collective-permute-done | bytes 524320 | tf_op jit(solution)/shard_map/ppermute | solution.py:35
  22.8 3.3 %collective-permute-done.2.refs_2_ = bf16[256,1024]{1,0:T(8,128)(2,1)S(1)} collective-permute-done((bf16[256,1024]{1,0:T(8,128)(2,1)}, bf16[256,1024]{1,0:T(8,128)(2,1)S(1)}, u32[]{:S(2)}, u32[]{:S(2)}) %collective-permute-start.2) | collective-permute-done | bytes 524320 | tf_op jit(solution)/shard_map/ppermute | solution.py:35
  26.1 2.5 %broadcast_in_dim.34 = bf16[8,256,1024]{2,1,0:T(8,128)(2,1)} broadcast(bf16[256,1024]{1,0:T(8,128)(2,1)S(1)} %bitcast.40), dimensions={1,2} | broadcast | bytes 4718592 | tf_op jit(solution)/shard_map/broadcast_in_dim | solution.py:647
  29.4 1.7 collective-permute-start.5
  31.8 6.4 %ln_proj.5 = (bf16[1024,2048]{1,0:T(8,128)(2,1)}, bf16[2,8,128,512]{3,2,1,0:T(8,128)(2,1)}, f32[2,8,128,512]{3,2,1,0:T(8,128)}) custom-call(s32[3]{0:T(128)} %get-tuple-element.157.at_ref, bf16[256,1024]{1,0:T(8,128)(2,1)} %copy-done.8, bf16[256,1024]{1,0:T(8,128)(2,1)} %copy-done.9, ...), custom_call_target="tpu_custom_call", output_to_operand_aliasing={{0}: (5, {}), {1}: (6, {}), {2}: (7, {})} | custom-call | flops 805306368 | bytes 9437184 | tf_op jit(solution)/shard_map/ln_proj/pallas_call | solution.py:144
  38.3 2.1 %collective-permute-done.5.refs_2_ = bf16[256,1024]{1,0:T(8,128)(2,1)S(1)} collective-permute-done((bf16[256,1024]{1,0:T(8,128)(2,1)S(1)}, bf16[256,1024]{1,0:T(8,128)(2,1)S(1)}, u32[]{:S(2)}, u32[]{:S(2)}) %collective-permute-start.5) | collective-permute-done | bytes 524320 | tf_op jit(solution)/shard_map/ppermute | solution.py:35
  40.5 0.9 collective-permute-start.6
  42.2 2.0 %collective-permute-start.8 = (bf16[80,1024]{1,0:T(8,128)(2,1)S(1)}, bf16[80,1024]{1,0:T(8,128)(2,1)S(1)}, u32[]{:S(2)}, u32[]{:S(2)}) collective-permute-start(bf16[80,1024]{1,0:T(8,128)(2,1)S(1)} %slice.20), channel_id=1, source_target_pairs={{96,0},{112,16},{0,32},{16,48},{32,64},{48,80},{64,96},{80,112},{9... | collective-permute-start | bytes 491528 | tf_op jit(solution)/shard_map/ppermute | solution.py:35
  44.3 2.5 %select_add_fusion = s32[16,128]{1,0:T(8,128)} fusion(s32[]{:T(128)} %get-tuple-element.149, s32[]{:T(128)} %get-tuple-element.150, s32[]{:T(128)} %get-tuple-element.148, s32[8,128]{1,0:T(8,128)S(1)} %bitcast.43, s32[8,128]{1,0:T(8,128)S(1)} %bitcast.45), kind=kLoop, calls=%fused_computation.6 | loop fusion | flops 18432 | bytes 16396 | tf_op jit(solution)/shard_map/add | solution.py:657
  46.8 6.3 %ln_proj.6 = (bf16[1024,2048]{1,0:T(8,128)(2,1)}, bf16[2,8,128,512]{3,2,1,0:T(8,128)(2,1)}, f32[2,8,128,512]{3,2,1,0:T(8,128)}) custom-call(s32[3]{0:T(128)} %get-tuple-element.158.at_ref, bf16[256,1024]{1,0:T(8,128)(2,1)} %copy-done.5, bf16[256,1024]{1,0:T(8,128)(2,1)} %copy-done.4, ...), custom_call_target="tpu_custom_call", output_to_operand_aliasing={{0}: (5, {}), {1}: (6, {}), {2}: (7, {})} | custom-call | flops 805306368 | bytes 9437184 | tf_op jit(solution)/shard_map/ln_proj/pallas_call | solution.py:144
  53.1 0.8 pad_maximum_fusion.2.refs_0_
  53.9 4.7 %all-to-all-start.1 = ((bf16[8,256,1024]{2,1,0:T(8,128)(2,1)}), bf16[8,256,1024]{2,1,0:T(8,128)(2,1)}, u32[]{:S(2)}, u32[]{:S(2)}) async-start(bf16[8,256,1024]{2,1,0:T(8,128)(2,1)} %broadcast_in_dim.34), calls=%async_computation.1 | async-start | bytes 8388608 | tf_op jit(solution)/shard_map/all_to_all | solution.py:659
  58.6 3.1 %ln_proj.7 = (bf16[1024,2048]{1,0:T(8,128)(2,1)}, bf16[2,8,128,512]{3,2,1,0:T(8,128)(2,1)}, f32[2,8,128,512]{3,2,1,0:T(8,128)}) custom-call(s32[1]{0:T(128)} %bitcast.5.at_ref, bf16[256,1024]{1,0:T(8,128)(2,1)} %pad_maximum_fusion.2.refs_0_, ...), custom_call_target="tpu_custom_call", output_to_operand_aliasing={{0}: (3, {}), {1}: (4, {}), {2}: (5, {})} | custom-call | flops 268435456 | bytes 3145728 | tf_op jit(solution)/shard_map/ln_proj/pallas_call | solution.py:144
  61.8 6.8 %attention_forward.1 = (f32[128,2048]{1,0:T(8,128)}, bf16[128,2048]{1,0:T(8,128)(2,1)}, bf16[128,2048]{1,0:T(8,128)(2,1)}, f32[4,2048]{1,0:T(4,128)}) custom-call(bf16[2,8,128,512]{3,2,1,0:T(8,128)(2,1)} %get-tuple-element.103.act_ref, bf16[8,272,128]{2,1,0:T(8,128)(2,1)} %copy-done.7, s32[1,2048]{1,0:T(1,128)} %bitcast.48), custom_call_target="tpu_custom_call" | custom-call | flops 4294967296 | bytes 6291456 | tf_op jit(solution)/shard_map/attention_forward/pallas_call | solution.py:247
  68.6 1.7 collective-permute-start.9
  70.3 30.6 %collective-permute-done.9 = f32[4,2048]{1,0:T(4,128)S(1)} collective-permute-done((f32[4,2048]{1,0:T(4,128)}, f32[4,2048]{1,0:T(4,128)S(1)}, u32[]{:S(2)}, u32[]{:S(2)}) %collective-permute-start.9) | collective-permute-done | bytes 32800 | tf_op jit(solution)/shard_map/ppermute | solution.py:35
  101.7 2.4 %collective-permute-start.10 = (f32[2,4,2048]{2,1,0:T(4,128)S(1)}, f32[2,4,2048]{2,1,0:T(4,128)S(1)}, u32[]{:S(2)}, u32[]{:S(2)}) collective-permute-start(f32[2,4,2048]{2,1,0:T(4,128)S(1)} %pad_maximum_fusion.3.own_ref), channel_id=1, source_target_pairs={{32,0},{48,16},{64,32},{80,48},{96,64},{112,80},{0,96},{16,112},{3... | collective-permute-start | bytes 196616 | tf_op jit(solution)/shard_map/ppermute | solution.py:35
  104.1 2.6 %collective-permute-start.12 = (f32[2,4,2048]{2,1,0:T(4,128)S(1)}, f32[2,4,2048]{2,1,0:T(4,128)S(1)}, u32[]{:S(2)}, u32[]{:S(2)}) collective-permute-start(f32[2,4,2048]{2,1,0:T(4,128)S(1)} %pad_maximum_fusion.3.own_ref), channel_id=1, source_target_pairs={{64,0},{80,16},{96,32},{112,48},{0,64},{16,80},{32,96},{48,112},{6... | collective-permute-start | bytes 196616 | tf_op jit(solution)/shard_map/ppermute | solution.py:35
  106.7 3.6 %collective-permute-done.11.three_ref = f32[2,4,2048]{2,1,0:T(4,128)S(1)} collective-permute-done((f32[2,4,2048]{2,1,0:T(4,128)S(1)}, f32[2,4,2048]{2,1,0:T(4,128)S(1)}, u32[]{:S(2)}, u32[]{:S(2)}) %collective-permute-start.11) | collective-permute-done | bytes 65568 | tf_op jit(solution)/shard_map/ppermute | solution.py:35
  111.0 4.2 %mix.1 = (bf16[8,256,256]{2,1,0:T(8,128)(2,1)}, bf16[2048,128]{1,0:T(8,128)(2,1)}, bf16[128,2048]{1,0:T(8,128)(2,1)}) custom-call(f32[2,4,2048]{2,1,0:T(4,128)} %copy-done.11, f32[2,4,2048]{2,1,0:T(4,128)} %copy-done.12, f32[2,4,2048]{2,1,0:T(4,128)} %copy-done.13, f32[2,4,2048]{2,1,0:T(4,128)} %copy-done.14, f32[128,2048]{1,0:T(8,128)} %get-tuple-element.107.att_ref, ...), custom_call_target="tpu_custom_call" | custom-call | flops 5242880 | bytes 6291456 | tf_op jit(solution)/shard_map/mix/pallas_call | solution.py:297
  115.2 15.2 %attention_backward.1.grad_ref.gated_ref = bf16[8,256,640]{2,1,0:T(8,128)(2,1)} custom-call(bf16[2,8,128,512]{3,2,1,0:T(8,128)(2,1)} %get-tuple-element.103.act_ref, bf16[2048,128]{1,0:T(8,128)(2,1)} %get-tuple-element.111.go_ref, bf16[128,2048]{1,0:T(8,128)(2,1)} %get-tuple-element.112.got_ref, s32[1,2048]{1,0:T(1,128)} %bitcast.49, ...), custom_call_target="tpu_custom_call" | custom-call | flops 8053063680 | bytes 10485760 | tf_op jit(solution)/shard_map/attention_backward/pallas_call | solution.py:375
  130.4 4.2 %all-to-all-start.2 = ((bf16[8,256,640]{2,1,0:T(8,128)(2,1)}), bf16[8,256,640]{2,1,0:T(8,128)(2,1)S(1)}, u32[]{:S(2)}, u32[]{:S(2)}) async-start(bf16[8,256,640]{2,1,0:T(8,128)(2,1)} %attention_backward.1.grad_ref.gated_ref), calls=%async_computation.2 | async-start | bytes 5242880 | tf_op jit(solution)/shard_map/all_to_all | solution.py:667
  134.6 6.5 %terms_in.1 = (f32[8,80,512]{2,1,0:T(8,128)}, f32[8,80,512]{2,1,0:T(8,128)}) custom-call(s32[1]{0:T(128)} %bitcast.4.core_ref, bf16[1024,2048]{1,0:T(8,128)(2,1)} %get-tuple-element.117.normed_ref, bf16[8,256,640]{2,1,0:T(8,128)(2,1)} %attention_backward.1.grad_ref.gated_ref), custom_call_target="tpu_custom_call" | custom-call | flops 2147483648 | bytes 9437184 | tf_op jit(solution)/shard_map/terms_in/pallas_call | solution.py:407
  141.2 3.6 %terms_out.1 = (f32[8,80,512]{2,1,0:T(8,128)}, f32[8,80,512]{2,1,0:T(8,128)}) custom-call(s32[1]{0:T(128)} %bitcast.4.core_ref, bf16[8,256,640]{2,1,0:T(8,128)(2,1)} %attention_backward.1.grad_ref.gated_ref, bf16[2048,1024]{1,0:T(8,128)(2,1)} %bitcast.22.cot_ref, f32[8,80,512]{2,1,0:T(8,128)} %get-tuple-element.118._, ...), custom_call_target="tpu_custom_call", output_to_operand_aliasing={{0}: (3, {}), {1}: (4, {})} | custom-call | flops 536870912 | bytes 6291456 | tf_op jit(solution)/shard_map/terms_out/pallas_call | solution.py:445
  145.4 2.7 %collective-permute-done.13.got_ref = f32[8,80,512]{2,1,0:T(8,128)} collective-permute-done((f32[8,80,512]{2,1,0:T(8,128)}, f32[8,80,512]{2,1,0:T(8,128)}, u32[]{:S(2)}, u32[]{:S(2)}) %collective-permute-start.13) | collective-permute-done | bytes 1310752 | tf_op jit(solution)/shard_map/ppermute | solution.py:39
  148.1 2.7 %core_sum.1 = (f32[2,80,512]{2,1,0:T(8,128)}, bf16[2,80,512]{2,1,0:T(8,128)(2,1)}, bf16[2,80,512]{2,1,0:T(8,128)(2,1)}, bf16[2,80,512]{2,1,0:T(8,128)(2,1)}) custom-call(s32[4]{0:T(128)} %pad_add_fusion.1.pos_ref, f32[8,80,512]{2,1,0:T(8,128)} %get-tuple-element.120.keep_ref, f32[8,80,512]{2,1,0:T(8,128)} %collective-permute-done.13.got_ref), custom_call_target="tpu_custom_call" | custom-call | flops 2621440 | bytes 5242880 | tf_op jit(solution)/shard_map/core_sum/pallas_call | solution.py:468
  150.9 3.0 %collective-permute-start.14 = (bf16[2,80,512]{2,1,0:T(8,128)(2,1)}, bf16[2,80,512]{2,1,0:T(8,128)(2,1)S(1)}, u32[]{:S(2)}, u32[]{:S(2)}) collective-permute-start(bf16[2,80,512]{2,1,0:T(8,128)(2,1)} %get-tuple-element.122), channel_id=1, source_target_pairs={{4,0},{5,1},{6,2},{7,3},{8,4},{9,5},{10,6},{11,7},{12,8},{13,9},{1... | collective-permute-start | bytes 491528 | tf_op jit(solution)/shard_map/ppermute | solution.py:39
  153.9 2.2 %collective-permute-start.16 = (bf16[2,80,512]{2,1,0:T(8,128)(2,1)}, bf16[2,80,512]{2,1,0:T(8,128)(2,1)S(1)}, u32[]{:S(2)}, u32[]{:S(2)}) collective-permute-start(bf16[2,80,512]{2,1,0:T(8,128)(2,1)} %get-tuple-element.124), channel_id=1, source_target_pairs={{8,0},{9,1},{10,2},{11,3},{12,4},{13,5},{14,6},{15,7},{0,8},{1,9},... | collective-permute-start | bytes 491528 | tf_op jit(solution)/shard_map/ppermute | solution.py:39
  156.1 4.7 %all-to-all-done.2.gated_ref.grad_ref = bf16[8,256,640]{2,1,0:T(8,128)(2,1)S(1)} async-done(((bf16[8,256,640]{2,1,0:T(8,128)(2,1)}), bf16[8,256,640]{2,1,0:T(8,128)(2,1)S(1)}, u32[]{:S(2)}, u32[]{:S(2)}) %all-to-all-start.2) | async-done | bytes 2621472 | tf_op jit(solution)/shard_map/all_to_all | solution.py:667
  160.8 1.5 copy-done.2
  162.3 6.2 %shard_out.1 = (bf16[256,1024]{1,0:T(8,128)(2,1)}, f32[256,1024]{1,0:T(8,128)}) custom-call(bf16[8,256,640]{2,1,0:T(8,128)(2,1)} %copy-done.2, bf16[8,256,640]{2,1,0:T(8,128)(2,1)} %copy-done.2, bf16[1024,4096]{1,0:T(8,128)(2,1)} %w_in_ref.3, bf16[1024,1024]{1,0:T(8,128)(2,1)} %w_out_ref.1, bf16[256,1024]{1,0:T(8,128)(2,1)} %bitcast.35), custom_call_target="tpu_custom_call" | custom-call | flops 1610612736 | bytes 8388608 | tf_op jit(solution)/shard_map/shard_out/pallas_call | solution.py:567
  169.2 3.0 %collective-permute-start.17 = (f32[48,512]{1,0:T(8,128)S(1)}, f32[48,512]{1,0:T(8,128)S(1)}, u32[]{:S(2)}, u32[]{:S(2)}) collective-permute-start(f32[48,512]{1,0:T(8,128)S(1)} %get-tuple-element.132), channel_id=1, source_target_pairs={{2,0},{3,1},{0,2},{1,3},{6,4},{7,5},{4,6},{5,7},{10,8},{11,9},{8,1... | collective-permute-start | bytes 294920 | tf_op jit(solution)/shard_map/ppermute | solution.py:47
  172.3 1.1 collective-permute-start.19
  173.4 5.5 %shard_grad.1 = bf16[256,1024]{1,0:T(8,128)(2,1)} custom-call(bf16[8,256,640]{2,1,0:T(8,128)(2,1)} %copy-done.2, bf16[1024,4096]{1,0:T(8,128)(2,1)} %w_in_ref.3, bf16[256,1024]{1,0:T(8,128)(2,1)} %bitcast.36, bf16[256,1024]{1,0:T(8,128)(2,1)} %bitcast.39, f32[256,1024]{1,0:T(8,128)} %get-tuple-element.135.half_ref), custom_call_target="tpu_custom_call" | custom-call | flops 1073741824 | bytes 8388608 | tf_op jit(solution)/shard_map/shard_grad/pallas_call | solution.py:590
  179.4 1.5 collective-permute-start.20
  181.5 1.0 collective-permute-start.22
  182.5 0.9 collective-permute-done.20.one_ref
  183.4 2.7 %collective-permute-done.21.three_ref = f32[16,512]{1,0:T(8,128)S(1)} collective-permute-done((f32[16,512]{1,0:T(8,128)S(1)}, f32[16,512]{1,0:T(8,128)S(1)}, u32[]{:S(2)}, u32[]{:S(2)}) %collective-permute-start.21) | collective-permute-done | bytes 32800 | tf_op jit(solution)/shard_map/ppermute | solution.py:35
  186.1 0.8 collective-permute-done.22.two_ref
  186.9 1.2 z_place.1
  (73 shorter events, 7.1 us)
Async XLA Ops:
  0.6 8.7 %copy-start.15 = (s32[1,256]{1,0:T(1,128)S(1)}, s32[1,256]{1,0:T(1,128)}, u32[]{:S(2)}) copy-start(s32[1,256]{1,0:T(1,128)} %param.6) | copy-start | bytes 3076
  0.6 19.6 %collective-permute-start = (bf16[256,1024]{1,0:T(8,128)(2,1)}, bf16[256,1024]{1,0:T(8,128)(2,1)S(1)}, u32[]{:S(2)}, u32[]{:S(2)}) collective-permute-start(bf16[256,1024]{1,0:T(8,128)(2,1)} %bitcast.31), channel_id=1, source_target_pairs={{16,0},{0,16},{48,32},{32,48},{80,64},{64,80},{112,96},{96,112},{1... | collective-permute-start | bytes 1572872 | tf_op jit(solution)/shard_map/ppermute | solution.py:35
  2.3 20.5 %collective-permute-start.1 = (bf16[256,1024]{1,0:T(8,128)(2,1)}, bf16[256,1024]{1,0:T(8,128)(2,1)S(1)}, u32[]{:S(2)}, u32[]{:S(2)}) collective-permute-start(bf16[256,1024]{1,0:T(8,128)(2,1)} %bitcast.32), channel_id=1, source_target_pairs={{32,0},{48,16},{64,32},{80,48},{96,64},{112,80},{0,96},{16,112},{3... | collective-permute-start | bytes 1572872 | tf_op jit(solution)/shard_map/ppermute | solution.py:35
  6.3 19.7 %collective-permute-start.2 = (bf16[256,1024]{1,0:T(8,128)(2,1)}, bf16[256,1024]{1,0:T(8,128)(2,1)S(1)}, u32[]{:S(2)}, u32[]{:S(2)}) collective-permute-start(bf16[256,1024]{1,0:T(8,128)(2,1)} %bitcast.33), channel_id=1, source_target_pairs={{96,0},{112,16},{0,32},{16,48},{32,64},{48,80},{64,96},{80,112},{9... | collective-permute-start | bytes 1572872 | tf_op jit(solution)/shard_map/ppermute | solution.py:35
  10.2 21.5 %all-to-all-start = ((bf16[8,272,128]{2,1,0:T(8,128)(2,1)}), bf16[8,272,128]{2,1,0:T(8,128)(2,1)S(1)}, u32[]{:S(2)}, u32[]{:S(2)}) async-start(bf16[8,272,128]{2,1,0:T(8,128)(2,1)} %pad_maximum_fusion.1), calls=%async_computation | async-start | bytes 1114112 | tf_op jit(solution)/shard_map/all_to_all | solution.py:646
  16.1 10.0 %copy-start.3 = (bf16[1,256,1024]{2,1,0:T(8,128)(2,1)S(1)}, bf16[1,256,1024]{2,1,0:T(8,128)(2,1)}, u32[]{:S(2)}) copy-start(bf16[1,256,1024]{2,1,0:T(8,128)(2,1)} %param.9) | copy-start | bytes 1572868
  20.3 9.1 %copy-start.8 = (bf16[256,1024]{1,0:T(8,128)(2,1)}, bf16[256,1024]{1,0:T(8,128)(2,1)S(1)}, u32[]{:S(2)}) copy-start(bf16[256,1024]{1,0:T(8,128)(2,1)S(1)} %collective-permute-done.refs_0_) | copy-start | bytes 1572868
  22.8 6.3 %copy-start.9 = (bf16[256,1024]{1,0:T(8,128)(2,1)}, bf16[256,1024]{1,0:T(8,128)(2,1)S(1)}, u32[]{:S(2)}) copy-start(bf16[256,1024]{1,0:T(8,128)(2,1)S(1)} %collective-permute-done.1.refs_1_) | copy-start | bytes 1572868
  26.1 2.5 %copy-start.10 = (bf16[256,1024]{1,0:T(8,128)(2,1)}, bf16[256,1024]{1,0:T(8,128)(2,1)S(1)}, u32[]{:S(2)}) copy-start(bf16[256,1024]{1,0:T(8,128)(2,1)S(1)} %collective-permute-done.2.refs_2_) | copy-start | bytes 1572868
  28.6 9.6 %collective-permute-start.3 = (bf16[256,1024]{1,0:T(8,128)(2,1)S(1)}, bf16[256,1024]{1,0:T(8,128)(2,1)S(1)}, u32[]{:S(2)}, u32[]{:S(2)}) collective-permute-start(bf16[256,1024]{1,0:T(8,128)(2,1)S(1)} %collective-permute-done.1.refs_1_), channel_id=1, source_target_pairs={{16,0},{0,16},{48,32},{32,48},{80,64},{64,80},{112,96},{96,112},{1... | collective-permute-start | bytes 1572872 | tf_op jit(solution)/shard_map/ppermute | solution.py:35
  29.1 9.2 %collective-permute-start.4 = (bf16[256,1024]{1,0:T(8,128)(2,1)S(1)}, bf16[256,1024]{1,0:T(8,128)(2,1)S(1)}, u32[]{:S(2)}, u32[]{:S(2)}) collective-permute-start(bf16[256,1024]{1,0:T(8,128)(2,1)S(1)} %collective-permute-done.1.refs_1_), channel_id=1, source_target_pairs={{32,0},{48,16},{64,32},{80,48},{96,64},{112,80},{0,96},{16,112},{3... | collective-permute-start | bytes 1572872 | tf_op jit(solution)/shard_map/ppermute | solution.py:35
  29.4 11.0 %collective-permute-start.5 = (bf16[256,1024]{1,0:T(8,128)(2,1)S(1)}, bf16[256,1024]{1,0:T(8,128)(2,1)S(1)}, u32[]{:S(2)}, u32[]{:S(2)}) collective-permute-start(bf16[256,1024]{1,0:T(8,128)(2,1)S(1)} %collective-permute-done.refs_0_), channel_id=1, source_target_pairs={{96,0},{112,16},{0,32},{16,48},{32,64},{48,80},{64,96},{80,112},{9... | collective-permute-start | bytes 1572872 | tf_op jit(solution)/shard_map/ppermute | solution.py:35
  31.7 6.4 %copy-start.7 = (bf16[8,272,128]{2,1,0:T(8,128)(2,1)}, bf16[8,272,128]{2,1,0:T(8,128)(2,1)S(1)}, u32[]{:S(2)}) copy-start(bf16[8,272,128]{2,1,0:T(8,128)(2,1)S(1)} %all-to-all-done.head_ref) | copy-start | bytes 1671172
  38.1 8.6 %copy-start.5 = (bf16[256,1024]{1,0:T(8,128)(2,1)}, bf16[256,1024]{1,0:T(8,128)(2,1)S(1)}, u32[]{:S(2)}) copy-start(bf16[256,1024]{1,0:T(8,128)(2,1)S(1)} %collective-permute-done.3.refs_0_) | copy-start | bytes 1572868
  38.3 8.5 %copy-start.4 = (bf16[256,1024]{1,0:T(8,128)(2,1)}, bf16[256,1024]{1,0:T(8,128)(2,1)S(1)}, u32[]{:S(2)}) copy-start(bf16[256,1024]{1,0:T(8,128)(2,1)S(1)} %collective-permute-done.4.refs_1_) | copy-start | bytes 1572868
  40.4 6.3 %copy-start.6 = (bf16[256,1024]{1,0:T(8,128)(2,1)}, bf16[256,1024]{1,0:T(8,128)(2,1)S(1)}, u32[]{:S(2)}) copy-start(bf16[256,1024]{1,0:T(8,128)(2,1)S(1)} %collective-permute-done.5.refs_2_) | copy-start | bytes 1572868
  40.5 12.6 %collective-permute-start.6 = (bf16[96,1024]{1,0:T(8,128)(2,1)S(1)}, bf16[96,1024]{1,0:T(8,128)(2,1)S(1)}, u32[]{:S(2)}, u32[]{:S(2)}) collective-permute-start(bf16[96,1024]{1,0:T(8,128)(2,1)S(1)} %slice.18), channel_id=1, source_target_pairs={{16,0},{0,16},{48,32},{32,48},{80,64},{64,80},{112,96},{96,112},{1... | collective-permute-start | bytes 589832 | tf_op jit(solution)/shard_map/ppermute | solution.py:35
  42.1 11.0 %collective-permute-start.7 = (bf16[80,1024]{1,0:T(8,128)(2,1)S(1)}, bf16[80,1024]{1,0:T(8,128)(2,1)S(1)}, u32[]{:S(2)}, u32[]{:S(2)}) collective-permute-start(bf16[80,1024]{1,0:T(8,128)(2,1)S(1)} %slice.19), channel_id=1, source_target_pairs={{32,0},{48,16},{64,32},{80,48},{96,64},{112,80},{0,96},{16,112},{3... | collective-permute-start | bytes 491528 | tf_op jit(solution)/shard_map/ppermute | solution.py:35
  42.2 10.8 %collective-permute-start.8 = (bf16[80,1024]{1,0:T(8,128)(2,1)S(1)}, bf16[80,1024]{1,0:T(8,128)(2,1)S(1)}, u32[]{:S(2)}, u32[]{:S(2)}) collective-permute-start(bf16[80,1024]{1,0:T(8,128)(2,1)S(1)} %slice.20), channel_id=1, source_target_pairs={{96,0},{112,16},{0,32},{16,48},{32,64},{48,80},{64,96},{80,112},{9... | collective-permute-start | bytes 491528 | tf_op jit(solution)/shard_map/ppermute | solution.py:35
  53.9 76.5 %all-to-all-start.1 = ((bf16[8,256,1024]{2,1,0:T(8,128)(2,1)}), bf16[8,256,1024]{2,1,0:T(8,128)(2,1)}, u32[]{:S(2)}, u32[]{:S(2)}) async-start(bf16[8,256,1024]{2,1,0:T(8,128)(2,1)} %broadcast_in_dim.34), calls=%async_computation.1 | async-start | bytes 8388608 | tf_op jit(solution)/shard_map/all_to_all | solution.py:659
  68.6 32.3 %collective-permute-start.9 = (f32[4,2048]{1,0:T(4,128)}, f32[4,2048]{1,0:T(4,128)S(1)}, u32[]{:S(2)}, u32[]{:S(2)}) collective-permute-start(f32[4,2048]{1,0:T(4,128)} %get-tuple-element.106), channel_id=1, source_target_pairs={{16,0},{0,16},{48,32},{32,48},{80,64},{64,80},{112,96},{96,112},{1... | collective-permute-start | bytes 98312 | tf_op jit(solution)/shard_map/ppermute | solution.py:35
  101.7 8.6 %copy-start.11 = (f32[2,4,2048]{2,1,0:T(4,128)}, f32[2,4,2048]{2,1,0:T(4,128)S(1)}, u32[]{:S(2)}) copy-start(f32[2,4,2048]{2,1,0:T(4,128)S(1)} %pad_maximum_fusion.3.own_ref) | copy-start | bytes 196612
  101.7 5.0 %collective-permute-start.10 = (f32[2,4,2048]{2,1,0:T(4,128)S(1)}, f32[2,4,2048]{2,1,0:T(4,128)S(1)}, u32[]{:S(2)}, u32[]{:S(2)}) collective-permute-start(f32[2,4,2048]{2,1,0:T(4,128)S(1)} %pad_maximum_fusion.3.own_ref), channel_id=1, source_target_pairs={{32,0},{48,16},{64,32},{80,48},{96,64},{112,80},{0,96},{16,112},{3... | collective-permute-start | bytes 196616 | tf_op jit(solution)/shard_map/ppermute | solution.py:35
  104.1 6.2 %collective-permute-start.11 = (f32[2,4,2048]{2,1,0:T(4,128)S(1)}, f32[2,4,2048]{2,1,0:T(4,128)S(1)}, u32[]{:S(2)}, u32[]{:S(2)}) collective-permute-start(f32[2,4,2048]{2,1,0:T(4,128)S(1)} %pad_maximum_fusion.3.own_ref), channel_id=1, source_target_pairs={{96,0},{112,16},{0,32},{16,48},{32,64},{48,80},{64,96},{80,112},{9... | collective-permute-start | bytes 196616 | tf_op jit(solution)/shard_map/ppermute | solution.py:35
  104.1 6.2 %collective-permute-start.12 = (f32[2,4,2048]{2,1,0:T(4,128)S(1)}, f32[2,4,2048]{2,1,0:T(4,128)S(1)}, u32[]{:S(2)}, u32[]{:S(2)}) collective-permute-start(f32[2,4,2048]{2,1,0:T(4,128)S(1)} %pad_maximum_fusion.3.own_ref), channel_id=1, source_target_pairs={{64,0},{80,16},{96,32},{112,48},{0,64},{16,80},{32,96},{48,112},{6... | collective-permute-start | bytes 196616 | tf_op jit(solution)/shard_map/ppermute | solution.py:35
  106.7 3.6 %copy-start.12 = (f32[2,4,2048]{2,1,0:T(4,128)}, f32[2,4,2048]{2,1,0:T(4,128)S(1)}, u32[]{:S(2)}) copy-start(f32[2,4,2048]{2,1,0:T(4,128)S(1)} %collective-permute-done.10.one_ref) | copy-start | bytes 196612
  110.3 0.6 copy-start.13
  110.3 0.7 copy-start.14
  130.4 30.4 %all-to-all-start.2 = ((bf16[8,256,640]{2,1,0:T(8,128)(2,1)}), bf16[8,256,640]{2,1,0:T(8,128)(2,1)S(1)}, u32[]{:S(2)}, u32[]{:S(2)}) async-start(bf16[8,256,640]{2,1,0:T(8,128)(2,1)} %attention_backward.1.grad_ref.gated_ref), calls=%async_computation.2 | async-start | bytes 5242880 | tf_op jit(solution)/shard_map/all_to_all | solution.py:667
  144.8 3.4 %collective-permute-start.13 = (f32[8,80,512]{2,1,0:T(8,128)}, f32[8,80,512]{2,1,0:T(8,128)}, u32[]{:S(2)}, u32[]{:S(2)}) collective-permute-start(f32[8,80,512]{2,1,0:T(8,128)} %get-tuple-element.121), channel_id=1, source_target_pairs={{1,0},{0,1},{3,2},{2,3},{5,4},{4,5},{7,6},{6,7},{9,8},{8,9},{11,10... | collective-permute-start | bytes 3932168 | tf_op jit(solution)/shard_map/ppermute | solution.py:39
  150.9 17.6 %collective-permute-start.14 = (bf16[2,80,512]{2,1,0:T(8,128)(2,1)}, bf16[2,80,512]{2,1,0:T(8,128)(2,1)S(1)}, u32[]{:S(2)}, u32[]{:S(2)}) collective-permute-start(bf16[2,80,512]{2,1,0:T(8,128)(2,1)} %get-tuple-element.122), channel_id=1, source_target_pairs={{4,0},{5,1},{6,2},{7,3},{8,4},{9,5},{10,6},{11,7},{12,8},{13,9},{1... | collective-permute-start | bytes 491528 | tf_op jit(solution)/shard_map/ppermute | solution.py:39
  153.9 14.6 %collective-permute-start.15 = (bf16[2,80,512]{2,1,0:T(8,128)(2,1)}, bf16[2,80,512]{2,1,0:T(8,128)(2,1)S(1)}, u32[]{:S(2)}, u32[]{:S(2)}) collective-permute-start(bf16[2,80,512]{2,1,0:T(8,128)(2,1)} %get-tuple-element.123), channel_id=1, source_target_pairs={{12,0},{13,1},{14,2},{15,3},{0,4},{1,5},{2,6},{3,7},{4,8},{5,9},{6... | collective-permute-start | bytes 491528 | tf_op jit(solution)/shard_map/ppermute | solution.py:39
  153.9 14.6 %copy-start = (f32[2,80,512]{2,1,0:T(8,128)S(1)}, f32[2,80,512]{2,1,0:T(8,128)}, u32[]{:S(2)}) copy-start(f32[2,80,512]{2,1,0:T(8,128)} %get-tuple-element.128.own_ref) | copy-start | bytes 983044
  153.9 14.6 %copy-start.1 = (s32[4]{0:T(128)S(1)}, s32[4]{0:T(128)}, u32[]{:S(2)}) copy-start(s32[4]{0:T(128)} %pad_add_fusion.1.pos_ref) | copy-start | bytes 52
  153.9 14.6 %collective-permute-start.16 = (bf16[2,80,512]{2,1,0:T(8,128)(2,1)}, bf16[2,80,512]{2,1,0:T(8,128)(2,1)S(1)}, u32[]{:S(2)}, u32[]{:S(2)}) collective-permute-start(bf16[2,80,512]{2,1,0:T(8,128)(2,1)} %get-tuple-element.124), channel_id=1, source_target_pairs={{8,0},{9,1},{10,2},{11,3},{12,4},{13,5},{14,6},{15,7},{0,8},{1,9},... | collective-permute-start | bytes 491528 | tf_op jit(solution)/shard_map/ppermute | solution.py:39
  160.8 1.5 copy-start.2
  169.2 9.7 %collective-permute-start.17 = (f32[48,512]{1,0:T(8,128)S(1)}, f32[48,512]{1,0:T(8,128)S(1)}, u32[]{:S(2)}, u32[]{:S(2)}) collective-permute-start(f32[48,512]{1,0:T(8,128)S(1)} %get-tuple-element.132), channel_id=1, source_target_pairs={{2,0},{3,1},{0,2},{1,3},{6,4},{7,5},{4,6},{5,7},{10,8},{11,9},{8,1... | collective-permute-start | bytes 294920 | tf_op jit(solution)/shard_map/ppermute | solution.py:47
  172.1 6.7 %collective-permute-start.18 = (f32[32,512]{1,0:T(8,128)S(1)}, f32[32,512]{1,0:T(8,128)S(1)}, u32[]{:S(2)}, u32[]{:S(2)}) collective-permute-start(f32[32,512]{1,0:T(8,128)S(1)} %get-tuple-element.133), channel_id=1, source_target_pairs={{16,0},{17,1},{18,2},{19,3},{20,4},{21,5},{22,6},{23,7},{24,8},{25... | collective-permute-start | bytes 196616 | tf_op jit(solution)/shard_map/ppermute | solution.py:47
  172.3 6.5 %collective-permute-start.19 = (f32[32,512]{1,0:T(8,128)S(1)}, f32[32,512]{1,0:T(8,128)S(1)}, u32[]{:S(2)}, u32[]{:S(2)}) collective-permute-start(f32[32,512]{1,0:T(8,128)S(1)} %get-tuple-element.134), channel_id=1, source_target_pairs={{18,0},{19,1},{16,2},{17,3},{22,4},{23,5},{20,6},{21,7},{26,8},{27... | collective-permute-start | bytes 196616 | tf_op jit(solution)/shard_map/ppermute | solution.py:47
  179.4 4.0 %collective-permute-start.20 = (f32[16,512]{1,0:T(8,128)S(1)}, f32[16,512]{1,0:T(8,128)S(1)}, u32[]{:S(2)}, u32[]{:S(2)}) collective-permute-start(f32[16,512]{1,0:T(8,128)S(1)} %get-tuple-element.142), channel_id=1, source_target_pairs={{32,0},{48,16},{64,32},{80,48},{96,64},{112,80},{0,96},{16,112},{3... | collective-permute-start | bytes 98312 | tf_op jit(solution)/shard_map/ppermute | solution.py:35
  181.0 5.1 %collective-permute-start.21 = (f32[16,512]{1,0:T(8,128)S(1)}, f32[16,512]{1,0:T(8,128)S(1)}, u32[]{:S(2)}, u32[]{:S(2)}) collective-permute-start(f32[16,512]{1,0:T(8,128)S(1)} %get-tuple-element.143), channel_id=1, source_target_pairs={{96,0},{112,16},{0,32},{16,48},{32,64},{48,80},{64,96},{80,112},{9... | collective-permute-start | bytes 98312 | tf_op jit(solution)/shard_map/ppermute | solution.py:35
  181.5 5.4 %collective-permute-start.22 = (f32[16,512]{1,0:T(8,128)S(1)}, f32[16,512]{1,0:T(8,128)S(1)}, u32[]{:S(2)}, u32[]{:S(2)}) collective-permute-start(f32[16,512]{1,0:T(8,128)S(1)} %get-tuple-element.144), channel_id=1, source_target_pairs={{64,0},{80,16},{96,32},{112,48},{0,64},{16,80},{32,96},{48,112},{6... | collective-permute-start | bytes 98312 | tf_op jit(solution)/shard_map/ppermute | solution.py:35
